TPU v7x, 256 devices: a whole 4x4x8 slice. The times are simulated.
256 devices in a mesh: row: 16 (over z, y_hi), col: 8 (over x, core), dp: 2 (over y_lo).
Axes of the slice: x: 4, y: 4 (y_hi: 2, y_lo: 2; y = y_hi * 2 + y_lo), z: 8, core: 2. Of those that a mesh axis runs over, the one named last changes fastest.
Arguments:
- tokens: bfloat16 [512, 8192], P(('col', 'dp'), 'row'), may hold values from -6 to 6
- cotangent: bfloat16 [512, 8192], P(('col', 'dp'), 'row'), may hold values from -6 to 6
- gate_blocks: bfloat16 [16, 8, 32, 128, 128], P('row', 'col'), may hold values from -0.125 to 0.125
- up_blocks: bfloat16 [16, 8, 32, 128, 128], P('row', 'col'), may hold values from -0.125 to 0.125
- down_blocks: bfloat16 [8, 16, 32, 128, 128], P('col', 'row'), may hold values from -0.09375 to 0.09375
- gate_slots: int32 [16, 8, 32], P('row', 'col'), may hold values from -1 to 63, as said below
- up_slots: int32 [16, 8, 32], P('row', 'col'), may hold values from -1 to 63, as said below
- down_slots: int32 [8, 16, 32], P('col', 'row'), may hold values from -1 to 63, as said below
Outputs:
- layer_out: bfloat16 [512, 8192], P(('col', 'dp'), 'row')
- token_grad: bfloat16 [512, 8192], P(('col', 'dp'), 'row')
- gate_grad: float32 [16, 8, 32, 128, 128], P('row', 'col', None, 'dp')
- up_grad: float32 [16, 8, 32, 128, 128], P('row', 'col', None, 'dp')
- down_grad: float32 [8, 16, 32, 128, 128], P('col', 'row', None, 'dp')
Inputs may be any that keep to these rules, and one draw needn't show every extreme that they name: `gate_slots`: every entry is -1 or a position within one device's tile of 4 x 16 blocks (block row times 16 plus block column); on each device the positions are distinct and come before the -1 entries; some device has all 32 slots filled. `up_slots`: as for gate_slots, drawn independently. `down_slots`: every entry is -1 or a position within one device's tile of 16 x 4 blocks (block row times 4 plus block column); on each device the positions are distinct and come before the -1 entries; some device has all 32 slots filled.
All inputs are finite; a program needn't handle non-finite values.
Results may differ from a plain program's by a relative error of at most 0.035.
Values may be sent and summed in bfloat16 or wider, within the bound.
A program may use at most 64 MiB of HBM per device.

v0:
```python
import jax
import jax.numpy as jnp
from jax import lax
from jax.sharding import PartitionSpec as P

FF = 16384


def slot_masks(slot_list, count_first, count_second):
    live_mask = slot_list >= 0
    position = jnp.where(live_mask, slot_list, 0)
    first_hot = (position[:, None] // count_second == jnp.arange(count_first)[None, :]) & live_mask[
        :, None
    ]
    second_hot = (
        position[:, None] % count_second == jnp.arange(count_second)[None, :]
    ) & live_mask[:, None]
    return (first_hot, second_hot)


def block_apply(activations, blocks, slot_list, count_first, count_second, transposed):
    block_size = blocks.shape[-1]
    row_count = activations.shape[0]
    first_hot, second_hot = slot_masks(slot_list, count_first, count_second)
    if transposed:
        in_hot, out_hot, form = (second_hot, first_hot, "stc,sbc->stb")
    else:
        in_hot, out_hot, form = (first_hot, second_hot, "stb,sbc->stc")
    shaped = activations.reshape(row_count, -1, block_size)
    picked = jnp.einsum("tnb,sn->stb", shaped, in_hot.astype(activations.dtype))
    product = jnp.einsum(form, picked, blocks, preferred_element_type=jnp.float32)
    upper_part = product.astype(jnp.bfloat16)
    lower_part = (product - upper_part.astype(jnp.float32)).astype(jnp.bfloat16)
    out_table = out_hot.astype(jnp.bfloat16)
    result = jnp.einsum("stc,sn->tnc", upper_part, out_table, preferred_element_type=jnp.float32)
    result = result + jnp.einsum(
        "stc,sn->tnc", lower_part, out_table, preferred_element_type=jnp.float32
    )
    return result.reshape(row_count, -1)


def weight_grad(left_side, right_side, slot_list, count_first, count_second):
    block_size = left_side.shape[1] // count_first
    row_count = left_side.shape[0]
    first_hot, second_hot = slot_masks(slot_list, count_first, count_second)
    left_pick = jnp.einsum(
        "tnb,sn->stb",
        left_side.reshape(row_count, count_first, block_size),
        first_hot.astype(left_side.dtype),
    )
    right_pick = jnp.einsum(
        "tnb,sn->stb",
        right_side.reshape(row_count, count_second, block_size),
        second_hot.astype(right_side.dtype),
    )
    return jnp.einsum("sta,stb->sab", left_pick, right_pick, preferred_element_type=jnp.float32)


def swiglu_back(grad_hidden, gate_sum, up_sum):
    sigma = jax.nn.sigmoid(gate_sum)
    grad_gate = (grad_hidden * up_sum * sigma * (1.0 + gate_sum * (1.0 - sigma))).astype(
        jnp.bfloat16
    )
    grad_up = (grad_hidden * gate_sum * sigma).astype(jnp.bfloat16)
    return (grad_gate, grad_up)


def per_device(
    tokens, cotangent, gate_blocks, up_blocks, down_blocks, gate_slots, up_slots, down_slots
):
    block_size = gate_blocks.shape[-1]
    width_blocks = tokens.shape[1] // block_size
    hidden_blocks = FF // block_size // lax.axis_size("col")
    gate_tile, up_tile, down_tile = (gate_blocks[0, 0], up_blocks[0, 0], down_blocks[0, 0])
    gate_list, up_list, down_list = (gate_slots[0, 0], up_slots[0, 0], down_slots[0, 0])
    gathered = lax.all_gather(tokens, "col", axis=0, tiled=True)
    gate_part = block_apply(gathered, gate_tile, gate_list, width_blocks, hidden_blocks, False)
    up_part = block_apply(gathered, up_tile, up_list, width_blocks, hidden_blocks, False)
    gate_sum, up_sum = (
        lax.psum_scatter(
            gate_part.astype(jnp.bfloat16), "row", scatter_dimension=0, tiled=True
        ).astype(jnp.float32),
        lax.psum_scatter(
            up_part.astype(jnp.bfloat16), "row", scatter_dimension=0, tiled=True
        ).astype(jnp.float32),
    )
    hidden = (jax.nn.silu(gate_sum) * up_sum).astype(jnp.bfloat16)
    hidden_full = lax.all_gather(hidden, "row", axis=0, tiled=True)
    portion = hidden_full
    layer_sum = lax.psum_scatter(
        block_apply(portion, down_tile, down_list, hidden_blocks, width_blocks, False).astype(
            jnp.bfloat16
        ),
        "col",
        scatter_dimension=0,
        tiled=True,
    )
    cotangent_full = lax.all_gather(cotangent, "col", axis=0, tiled=True)
    portion = cotangent_full
    grad_hidden = lax.psum_scatter(
        block_apply(portion, down_tile, down_list, hidden_blocks, width_blocks, True).astype(
            jnp.bfloat16
        ),
        "row",
        scatter_dimension=0,
        tiled=True,
    ).astype(jnp.float32)
    grad_gate, grad_up = swiglu_back(grad_hidden, gate_sum, up_sum)
    gate_full, up_full = (
        lax.all_gather(grad_gate, "row", axis=0, tiled=True),
        lax.all_gather(grad_up, "row", axis=0, tiled=True),
    )
    first_term = block_apply(gate_full, gate_tile, gate_list, width_blocks, hidden_blocks, True)
    second_term = block_apply(up_full, up_tile, up_list, width_blocks, hidden_blocks, True)
    token_grad = lax.psum_scatter(
        (first_term + second_term).astype(jnp.bfloat16), "col", scatter_dimension=0, tiled=True
    )
    gate_local = weight_grad(gathered, gate_full, gate_list, width_blocks, hidden_blocks)
    up_local = weight_grad(gathered, up_full, up_list, width_blocks, hidden_blocks)
    down_local = weight_grad(hidden_full, cotangent_full, down_list, hidden_blocks, width_blocks)
    gate_grad, up_grad, down_grad = (
        lax.psum_scatter(
            gate_local.astype(jnp.bfloat16), "dp", scatter_dimension=1, tiled=True
        ).astype(jnp.float32),
        lax.psum_scatter(
            up_local.astype(jnp.bfloat16), "dp", scatter_dimension=1, tiled=True
        ).astype(jnp.float32),
        lax.psum_scatter(
            down_local.astype(jnp.bfloat16), "dp", scatter_dimension=1, tiled=True
        ).astype(jnp.float32),
    )
    return (
        layer_sum,
        token_grad,
        gate_grad[None, None],
        up_grad[None, None],
        down_grad[None, None],
    )


def solution(mesh):
    in_specs = (
        P(("col", "dp"), "row"),
        P(("col", "dp"), "row"),
        P("row", "col", None, None, None),
        P("row", "col", None, None, None),
        P("col", "row", None, None, None),
        P("row", "col", None),
        P("row", "col", None),
        P("col", "row", None),
    )
    out_specs = (
        P(("col", "dp"), "row"),
        P(("col", "dp"), "row"),
        P("row", "col", None, "dp", None),
        P("row", "col", None, "dp", None),
        P("col", "row", None, "dp", None),
    )
    return jax.shard_map(
        per_device, mesh=mesh, in_specs=in_specs, out_specs=out_specs, check_vma=False
    )
```

profile of v0, /device:TPU:8, one launch (start us, length us, event | category | flops | bytes accessed | tf_op | source)
XLA Modules:
  0.0 1048.5 jit_solution(341029386348062382)
XLA Ops:
  9.3 13.4 %all_gather.15 = bf16[256,512]{1,0:T(8,128)(2,1)S(1)} all-gather(bf16[32,512]{1,0:T(8,128)(2,1)} %param.8), channel_id=1, replica_groups=mesh['row'=16,'col'=8,'dp'=2] {'col'}, dimensions={0}, use_global_device_ids=true | all-gather | bytes 294912 | tf_op jit(solution)/shard_map/all_gather | solution.py:76
  22.7 2.1 fusion.136
  24.9 3.0 copy.31
  27.9 2.2 subtract_convert_fusion.5
  30.1 1.3 fusion.20
  31.3 1.4 add_convert_fusion.2
  34.1 2.1 fusion.132
  36.2 4.3 copy.33
  40.5 2.8 subtract_convert_fusion.4
  43.3 1.3 fusion.16
  44.6 1.4 add_convert_fusion.1
  47.3 14.1 %all_gather.17 = bf16[256,512]{1,0:T(8,128)(2,1)} all-gather(bf16[32,512]{1,0:T(8,128)(2,1)S(1)} %copy-done.12), channel_id=1, replica_groups=mesh['row'=16,'col'=8,'dp'=2] {'col'}, dimensions={0}, use_global_device_ids=true | all-gather | bytes 294912 | tf_op jit(solution)/shard_map/all_gather | solution.py:98
  63.3 1.3 subtract_convert_fusion.2
  64.6 1.3 fusion.8
  65.9 1.3 add_convert_fusion
  68.6 169.8 %reduce-scatter.9.cloned.1.call-done = bf16[16,2048]{1,0:T(8,128)(2,1)} async-done(((bf16[256,2048]{1,0:T(8,128)(2,1)}), bf16[16,2048]{1,0:T(8,128)(2,1)}) %reduce-scatter.9.cloned.1.call-update) | async-done | bytes 65552 | tf_op jit(solution)/shard_map/reduce_scatter | solution.py:80
  238.4 205.1 %reduce-scatter.11.cloned.1.call-done = bf16[16,2048]{1,0:T(8,128)(2,1)} async-done(((bf16[256,2048]{1,0:T(8,128)(2,1)}), bf16[16,2048]{1,0:T(8,128)(2,1)}) %reduce-scatter.11.cloned.1.call-update) | async-done | bytes 65552 | tf_op jit(solution)/shard_map/reduce_scatter | solution.py:83
  443.5 205.3 %reduce-scatter.15.cloned.1.call-done = bf16[16,2048]{1,0:T(8,128)(2,1)} async-done(((bf16[256,2048]{1,0:T(8,128)(2,1)}), bf16[16,2048]{1,0:T(8,128)(2,1)}) %reduce-scatter.15.cloned.1.call-update) | async-done | bytes 65552 | tf_op jit(solution)/shard_map/reduce_scatter | solution.py:100
  648.8 1.6 fusion.81
  651.6 76.9 %all-gather.8.cloned.1.call-done = bf16[256,2048]{1,0:T(8,128)(2,1)} async-done(((bf16[16,2048]{1,0:T(8,128)(2,1)}), bf16[256,2048]{1,0:T(8,128)(2,1)}) %all-gather.8.cloned.1.call-update) | async-done | bytes 1048592 | tf_op jit(solution)/shard_map/all_gather | solution.py:111
  728.6 1.5 copy.43
  730.8 1.4 copy-done.4
  732.2 2.4 fusion.48
  734.6 72.3 %all-gather.6.cloned.1.call-done = bf16[256,2048]{1,0:T(8,128)(2,1)} async-done(((bf16[16,2048]{1,0:T(8,128)(2,1)}), bf16[256,2048]{1,0:T(8,128)(2,1)}) %all-gather.6.cloned.1.call-update) | async-done | bytes 1048592 | tf_op jit(solution)/shard_map/all_gather | solution.py:110
  807.0 1.5 copy.42
  809.2 1.3 copy-done.6
  810.5 2.4 fusion.45
  813.2 72.2 %all-gather.4.cloned.1.call-done = bf16[256,2048]{1,0:T(8,128)(2,1)} async-done(((bf16[16,2048]{1,0:T(8,128)(2,1)}), bf16[256,2048]{1,0:T(8,128)(2,1)}) %all-gather.4.cloned.1.call-update) | async-done | bytes 1048592 | tf_op jit(solution)/shard_map/all_gather | solution.py:88
  885.4 1.4 copy.39
  886.8 2.1 fusion.104
  888.9 4.5 copy.35
  893.4 4.0 fusion.42
  897.5 2.6 subtract_convert_fusion.3
  900.1 1.3 fusion.12
  901.3 1.3 fusion.66
  903.4 2.7 subtract_convert_fusion
  906.1 2.0 fusion
  908.1 3.3 subtract_convert_fusion.1
  911.8 3.1 fusion.60
  914.9 1.3 fusion.4
  916.5 1.3 fusion.63
  918.6 2.1 bitcast_convert_fusion.1
  920.7 19.0 %reduce-scatter.19.cloned.1.call-done = bf16[32,64,128]{2,1,0:T(8,128)(2,1)} async-done(((bf16[32,128,128]{2,1,0:T(8,128)(2,1)}), bf16[32,64,128]{2,1,0:T(8,128)(2,1)}) %reduce-scatter.19.cloned.1.call-update) | async-done | bytes 524304 | tf_op jit(solution)/shard_map/reduce_scatter | solution.py:122
  939.7 2.1 bitcast_convert_fusion.2
  941.9 26.8 %reduce-scatter.23.cloned.1.call-done = bf16[32,64,128]{2,1,0:T(8,128)(2,1)} async-done(((bf16[32,128,128]{2,1,0:T(8,128)(2,1)}), bf16[32,64,128]{2,1,0:T(8,128)(2,1)}) %reduce-scatter.23.cloned.1.call-update) | async-done | bytes 524304 | tf_op jit(solution)/shard_map/reduce_scatter | solution.py:128
  968.6 2.1 bitcast_convert_fusion
  970.8 36.2 %reduce-scatter.13.cloned.1.call-done = bf16[32,512]{1,0:T(8,128)(2,1)} async-done(((bf16[256,512]{1,0:T(8,128)(2,1)}), bf16[32,512]{1,0:T(8,128)(2,1)}) %reduce-scatter.13.cloned.1.call-update) | async-done | bytes 32784 | tf_op jit(solution)/shard_map/reduce_scatter | solution.py:90
  1007.0 35.0 %reduce-scatter.17.cloned.1.call-done = bf16[32,512]{1,0:T(8,128)(2,1)} async-done(((bf16[256,512]{1,0:T(8,128)(2,1)}), bf16[32,512]{1,0:T(8,128)(2,1)}) %reduce-scatter.17.cloned.1.call-update) | async-done | bytes 32784 | tf_op jit(solution)/shard_map/reduce_scatter | solution.py:115
  (70 shorter events, 13.3 us)
Async XLA Ops:
  7.2 56.1 %copy-start = (bf16[1,1,32,128,128]{4,3,2,1,0:T(8,128)(2,1)S(1)}, bf16[1,1,32,128,128]{4,3,2,1,0:T(8,128)(2,1)}, u32[]{:S(2)}) copy-start(bf16[1,1,32,128,128]{4,3,2,1,0:T(8,128)(2,1)} %param.12) | copy-start | bytes 3145732
  7.2 231.2 %reduce-scatter.9.cloned.1.call-start = ((), (), s32[]{:S(2)}) async-start(), calls=%async_computation.8 | async-start | bytes 1114112 | tf_op jit(solution)/shard_map/reduce_scatter | solution.py:80
  32.7 1.3 copy-start.13
  34.0 409.5 %reduce-scatter.11.cloned.1.call-start = ((), (), s32[]{:S(2)}) async-start(), calls=%async_computation.9 | async-start | bytes 1114112 | tf_op jit(solution)/shard_map/reduce_scatter | solution.py:83
  46.0 1.3 copy-start.12
  46.0 16.5 %copy-start.14 = (s32[1,1,32]{2,1,0:T(1,128)S(1)}, s32[1,1,32]{2,1,0:T(1,128)}, u32[]{:S(2)}) copy-start(s32[1,1,32]{2,1,0:T(1,128)} %param.15) | copy-start | bytes 388
  47.3 601.5 %reduce-scatter.15.cloned.1.call-start = ((), (), s32[]{:S(2)}) async-start(), calls=%async_computation.12 | async-start | bytes 1114112 | tf_op jit(solution)/shard_map/reduce_scatter | solution.py:100
  63.3 1.4 copy-start.1
  68.5 660.1 %all-gather.8.cloned.1.call-start = ((), (), s32[]{:S(2)}) async-start(), calls=%async_computation.14 | async-start | bytes 1114112 | tf_op jit(solution)/shard_map/all_gather | solution.py:111
  650.4 156.5 %all-gather.6.cloned.1.call-start = ((), (), s32[]{:S(2)}) async-start(), calls=%async_computation.13 | async-start | bytes 1114112 | tf_op jit(solution)/shard_map/all_gather | solution.py:110
  651.0 234.3 %all-gather.4.cloned.1.call-start = ((), (), s32[]{:S(2)}) async-start(), calls=%async_computation.10 | async-start | bytes 1114112 | tf_op jit(solution)/shard_map/all_gather | solution.py:88
  651.6 267.0 %reduce-scatter.21.cloned.1.call-start = ((), (), s32[]{:S(2)}) async-start(), calls=%async_computation.17 | async-start | bytes 1572864 | tf_op jit(solution)/shard_map/reduce_scatter | solution.py:125
  730.0 2.1 copy-start.3
  730.8 1.4 copy-start.4
  734.6 205.2 %reduce-scatter.19.cloned.1.call-start = ((), (), s32[]{:S(2)}) async-start(), calls=%async_computation.16 | async-start | bytes 1572864 | tf_op jit(solution)/shard_map/reduce_scatter | solution.py:122
  809.2 1.3 copy-start.6
  812.9 155.7 %reduce-scatter.23.cloned.1.call-start = ((), (), s32[]{:S(2)}) async-start(), calls=%async_computation.18 | async-start | bytes 1572864 | tf_op jit(solution)/shard_map/reduce_scatter | solution.py:128
  888.9 4.5 copy-start.2
  897.5 109.5 %reduce-scatter.13.cloned.1.call-start = ((), (), s32[]{:S(2)}) async-start(), calls=%async_computation.11 | async-start | bytes 294912 | tf_op jit(solution)/shard_map/reduce_scatter | solution.py:90
  901.3 2.1 copy-start.5
  901.3 2.1 copy-start.10
  903.4 4.7 copy-start.11
  906.1 2.0 copy-start.7
  911.5 130.5 %reduce-scatter.17.cloned.1.call-start = ((), (), s32[]{:S(2)}) async-start(), calls=%async_computation.15 | async-start | bytes 294912 | tf_op jit(solution)/shard_map/reduce_scatter | solution.py:115
  911.8 3.1 copy-start.9
  914.9 1.6 copy-start.8
Sparse Core Ops, SparseCore 0:
  34.1 204.2 reduce-scatter.8
  242.8 200.6 reduce-scatter.10
  447.9 200.8 reduce-scatter.14
  651.8 76.7 all-gather.7
  731.6 75.3 all-gather.5
  810.0 75.3 all-gather.3
  888.4 21.6 reduce-scatter.20
  913.3 26.3 reduce-scatter.18
  942.2 26.3 reduce-scatter.22
  971.7 35.2 reduce-scatter.12
  1010.1 31.8 reduce-scatter.16
where the time goes:
time: 1050 us
  waiting for transfers between devices  920 us (88%)
  matrix products  50.4 us (5%)
  blocking collectives  27.5 us (3%)
  local copies, waits for them, and re-layouts  25.5 us (2%)
  between operations  14.2 us (1%)
    reduce_scatter x2, waiting for transfers between devices, per_device(): lax.psum_scatter(block_apply(portion, down_tile, down_list, hidden_blocks...  241 us
    reduce_scatter x1, waiting for transfers between devices, per_device(): lax.psum_scatter(up_part.astype(jnp.bfloat16), 'row', scatter_dimension=0...  205 us
    reduce_scatter x1, waiting for transfers between devices, per_device(): lax.psum_scatter(gate_part.astype(jnp.bfloat16), 'row', scatter_dimension...  170 us
    all_gather x1, waiting for transfers between devices, per_device(): lax.all_gather(grad_up, 'row', axis=0, tiled=True)  76.9 us
    all_gather x1, waiting for transfers between devices, per_device(): lax.all_gather(grad_gate, 'row', axis=0, tiled=True)  72.3 us
    all_gather x1, waiting for transfers between devices, per_device(): hidden_full = lax.all_gather(hidden, 'row', axis=0, tiled=True)  72.2 us
    reduce_scatter x1, waiting for transfers between devices, per_device(): lax.psum_scatter((first_term + second_term).astype(jnp.bfloat16), 'col',...  35 us
    reduce_scatter x1, waiting for transfers between devices, per_device(): lax.psum_scatter(down_local.astype(jnp.bfloat16), 'dp', scatter_dimension...  26.8 us
  transfers between devices with their start and end apart: 11, of which 10 were waited for; matrix products, arithmetic and copies ran while one was open for 6% of the time, Pallas kernels for 0%

commit v1 on v0

v1 whole, which is shorter than its diff:
```python
import functools

import jax
import jax.numpy as jnp
from jax import lax
from jax.experimental import pallas as pl
from jax.experimental.pallas import tpu as pltpu
from jax.sharding import PartitionSpec as P

FF = 16384
BLK = 128
UNITS = 2
MESH = pl.DeviceIdType.MESH
F32 = jnp.float32
BF16 = jnp.bfloat16


def dot(a, b):
    return lax.dot_general(a, b, (((1,), (0,)), ((), ())), preferred_element_type=F32)


def dot_t(a, b):
    return lax.dot_general(a, b, (((1,), (1,)), ((), ())), preferred_element_type=F32)


def al(value, step):
    return pl.multiple_of(value, step)


def kernel(
    dims,
    slots_ref,
    inv_ref,
    tok_in,
    cot_in,
    gate_in,
    up_in,
    down_in,
    layer_out,
    tgrad_out,
    gate_out,
    up_out,
    down_out,
    blocks,
    tcg,
    wg,
    wu,
    wd,
    part,
    rs_send,
    rs_recv,
    y_send,
    y_recv,
    y_own,
    act,
    tok_t,
    hid_t,
    dense,
    dp_send,
    dp_recv,
    dp_own,
    col_part,
    ca_send,
    ca_recv,
    cb_send,
    cb_recv,
    col_stage,
    loc_sem,
    out_sem,
    p1_s,
    p1_r,
    rs_s,
    rs_r,
    ys_s,
    ys_r,
    ya_s,
    ya_r,
    ag_s,
    ag_r,
    dp_s,
    dp_r,
    ca_s,
    ca_r,
    cb_s,
    cb_r,
):
    n_row, n_col, n_tok, width, hid, cap = dims
    nz, nx = n_row // 2, n_col // 2
    steps = nz // 2
    group = n_tok * n_col
    zrows = group // nz
    own_rows = zrows // 2
    cw = hid // UNITS
    half = cw // 2
    drb, fcb = width // BLK, hid // BLK

    row, col, dp = lax.axis_index("row"), lax.axis_index("col"), lax.axis_index("dp")
    z, yh = lax.div(row, 2), lax.rem(row, 2)
    x, core = lax.div(col, 2), lax.rem(col, 2)
    z_right = (lax.rem(z + 1, nz) * 2 + yh, col, dp)
    z_left = (lax.rem(z + nz - 1, nz) * 2 + yh, col, dp)
    z_dev = (z_right, z_left)
    y_dev = (z * 2 + 1 - yh, col, dp)
    sib = (row, x * 2 + 1 - core, dp)
    dp_dev = (row, col, 1 - dp)

    def x_dev(k):
        return (row, lax.rem(x + k, nx) * 2 + core, dp)

    sends = []

    def send(src, dst, s_sem, r_sem, dev):
        copy = pltpu.make_async_remote_copy(
            src_ref=src, dst_ref=dst, send_sem=s_sem, recv_sem=r_sem, device_id=dev, device_id_type=MESH
        )
        copy.start()
        sends.append(copy)

    def arrived(dst, s_sem, r_sem, dev):
        pltpu.make_async_remote_copy(
            src_ref=dst, dst_ref=dst, send_sem=s_sem, recv_sem=r_sem, device_id=dev, device_id_type=MESH
        ).wait_recv()

    def tok_rows(c):
        return tcg.at[:, pl.ds(al(c * n_tok, n_tok), n_tok), :]

    mine = pl.ds(al(col * n_tok, n_tok), n_tok)
    own_loads = [
        pltpu.make_async_copy(tok_in, tcg.at[0, mine, :], loc_sem.at[0]),
        pltpu.make_async_copy(cot_in, tcg.at[1, mine, :], loc_sem.at[1]),
    ]
    block_loads = [
        pltpu.make_async_copy(ref, blocks.at[i, pl.ds(0, cap)], loc_sem.at[2 + i])
        for i, ref in enumerate((gate_in, up_in, down_in))
    ]
    for c in own_loads + block_loads:
        c.start()

    barrier = pltpu.get_barrier_semaphore()
    peers = [z_right, z_left, y_dev, sib, dp_dev] + [x_dev(k) for k in range(1, nx)]
    for dev in peers:
        pl.semaphore_signal(barrier, inc=1, device_id=dev, device_id_type=MESH)
    pl.semaphore_wait(barrier, len(peers))

    for c in own_loads:
        c.wait()
    send(tok_rows(col), tok_rows(col), p1_s.at[0], p1_r.at[0], sib)
    for k in range(1, nx):
        send(tok_rows(col), tok_rows(col), p1_s.at[k], p1_r.at[k], x_dev(k))

    for c in block_loads:
        c.wait()
    for i in range(3):
        blocks[i, cap] = jnp.zeros((BLK, BLK), BF16)
    dense[drb * fcb] = jnp.zeros((BLK, BLK), F32)

    def place(p, carry):
        r0, c0 = al((p // fcb) * BLK, BLK), al((p % fcb) * BLK, BLK)
        wg[pl.ds(r0, BLK), pl.ds(c0, BLK)] = blocks[0, inv_ref[0, p]]
        wu[pl.ds(r0, BLK), pl.ds(c0, BLK)] = blocks[1, inv_ref[1, p]]
        r1, c1 = al((p // drb) * BLK, BLK), al((p % drb) * BLK, BLK)
        wd[pl.ds(r1, BLK), pl.ds(c1, BLK)] = blocks[2, inv_ref[2, p]]
        return carry

    lax.fori_loop(0, drb * fcb, place, 0)

    for k in range(1, nx):
        src = lax.rem(x + nx - k, nx) * 2 + core
        arrived(tok_rows(src), p1_s.at[k], p1_r.at[k], sib)
        send(tok_rows(src), tok_rows(src), p1_s.at[nx + k - 1], p1_r.at[nx + k - 1], sib)
    arrived(tok_rows(x * 2 + 1 - core), p1_s.at[0], p1_r.at[0], sib)
    for k in range(1, nx):
        src = lax.rem(x + nx - k, nx) * 2 + 1 - core
        arrived(tok_rows(src), p1_s.at[nx + k - 1], p1_r.at[nx + k - 1], sib)

    def z_rows(t):
        return al(lax.rem(t + 2 * nz, nz) * zrows, zrows)

    def rs_cols(d, k):
        if k == 0:
            return pl.ds(d * half, half)
        return pl.ds(0, cw)

    def rs_start(u, d, k):
        target = z + (steps - k) * (1 - 2 * d)
        r0 = z_rows(target)
        for t in range(3):
            for h in range(2):
                if k == 0 and h != d:
                    continue
                value = part[t, pl.ds(r0, zrows), pl.ds(u * cw + h * half, half)]
                if k > 1 or (k == 1 and h == d):
                    value = value + rs_recv[u, d, k - 1, t, :, pl.ds(h * half, half)].astype(F32)
                rs_send[u, d, k, t, :, pl.ds(h * half, half)] = value.astype(BF16)
        c = rs_cols(d, k)
        send(
            rs_send.at[u, d, k, :, :, c],
            rs_recv.at[u, d, k, :, :, c],
            rs_s.at[u, d, k],
            rs_r.at[u, d, k],
            z_dev[d],
        )

    def rs_wait(u, d, k):
        arrived(rs_recv.at[u, d, k, :, :, rs_cols(d, k)], rs_s.at[u, d, k], rs_r.at[u, d, k], z_dev[d])

    tile = min(256, cw)
    for u in range(UNITS):

        def product(j, carry):
            c0 = al(u * cw + j * tile, tile)
            part[0, :, pl.ds(c0, tile)] = dot(tcg[0], wg[:, pl.ds(c0, tile)])
            part[1, :, pl.ds(c0, tile)] = dot(tcg[0], wu[:, pl.ds(c0, tile)])
            part[2, :, pl.ds(c0, tile)] = dot_t(tcg[1], wd[pl.ds(c0, tile), :])
            return carry

        lax.fori_loop(0, cw // tile, product, 0)
        for d in range(2):
            rs_start(u, d, 0)

    tok_t[...] = tcg[0].astype(F32).T.astype(BF16)

    for k in range(1, steps):
        for u in range(UNITS):
            for d in range(2):
                rs_wait(u, d, k - 1)
                rs_start(u, d, k)

    mine_r = al(z * zrows + yh * own_rows, own_rows)
    theirs_r = al(z * zrows + (1 - yh) * own_rows, own_rows)
    mine_o, theirs_o = al(yh * own_rows, own_rows), al((1 - yh) * own_rows, own_rows)
    zchunk = pl.ds(z_rows(z), zrows)

    for u in range(UNITS):
        for d in range(2):
            rs_wait(u, d, steps - 1)
        for t in range(3):

            def total(r0, o0):
                value = part[t, pl.ds(r0, own_rows), pl.ds(u * cw, cw)]
                for d in range(2):
                    value = value + rs_recv[u, d, steps - 1, t, pl.ds(o0, own_rows), :].astype(F32)
                return value

            y_send[u, t] = total(theirs_r, theirs_o).astype(BF16)
            y_own[u, t] = total(mine_r, mine_o)
        send(y_send.at[u], y_recv.at[u], ys_s.at[u], ys_r.at[u], y_dev)

    def act_rows(r0, u):
        return act.at[:, pl.ds(r0, own_rows), pl.ds(u * cw, cw)]

    for u in range(UNITS):
        arrived(y_recv.at[u], ys_s.at[u], ys_r.at[u], y_dev)
        for q in range(2):
            cs = pl.ds(q * half, half)
            gate = y_own[u, 0, :, cs] + y_recv[u, 0, :, cs].astype(F32)
            up = y_own[u, 1, :, cs] + y_recv[u, 1, :, cs].astype(F32)
            grad = y_own[u, 2, :, cs] + y_recv[u, 2, :, cs].astype(F32)
            sg = 1.0 / (1.0 + jnp.exp(-gate))
            co = pl.ds(u * cw + q * half, half)
            act[0, pl.ds(mine_r, own_rows), co] = (gate * sg * up).astype(BF16)
            act[1, pl.ds(mine_r, own_rows), co] = (
                grad * up * sg * (1.0 + gate * (1.0 - sg))
            ).astype(BF16)
            act[2, pl.ds(mine_r, own_rows), co] = (grad * gate * sg).astype(BF16)
        send(act_rows(mine_r, u), act_rows(mine_r, u), ya_s.at[u], ya_r.at[u], y_dev)

    def ag_slice(t, u, d, k, chunk):
        if k == steps - 1:
            c = pl.ds(u * cw + d * half, half)
        else:
            c = pl.ds(u * cw, cw)
        return act.at[t, pl.ds(z_rows(chunk), zrows), c]

    def ag_start(t, u, d, k):
        ref = ag_slice(t, u, d, k, z - k * (1 - 2 * d))
        send(ref, ref, ag_s.at[t, u, d, k], ag_r.at[t, u, d, k], z_dev[d])

    def ag_wait(t, u, d, k):
        ref = ag_slice(t, u, d, k, z - (k + 1) * (1 - 2 * d))
        arrived(ref, ag_s.at[t, u, d, k], ag_r.at[t, u, d, k], z_dev[d])

    def ag_step(t, k):
        for u in range(UNITS):
            if k == 0 and t == 0:
                arrived(act_rows(theirs_r, u), ya_s.at[u], ya_r.at[u], y_dev)
            for d in range(2):
                if k > 0:
                    ag_wait(t, u, d, k - 1)
                if k < steps:
                    ag_start(t, u, d, k)

    hb = BLK // 2

    def emit_blocks(i):
        def body(s, carry):
            value = dense[slots_ref[i, s]]
            low, high = value[:hb], value[hb:]
            dp_own[i, s] = jnp.where(dp == 0, low, high)
            dp_send[i, s] = jnp.where(dp == 0, high, low).astype(BF16)
            return carry

        lax.fori_loop(0, cap, body, 0)
        send(dp_send.at[i], dp_recv.at[i], dp_s.at[i], dp_r.at[i], dp_dev)

    out_copies = []

    def finish_blocks(i, out):
        arrived(dp_recv.at[i], dp_s.at[i], dp_r.at[i], dp_dev)

        def body(s, carry):
            dp_own[i, s] = dp_own[i, s] + dp_recv[i, s].astype(F32)
            return carry

        lax.fori_loop(0, cap, body, 0)
        copy = pltpu.make_async_copy(dp_own.at[i], out, out_sem.at[i])
        copy.start()
        out_copies.append(copy)

    def col_rows(c):
        return pl.ds(al(c * n_tok, n_tok), n_tok)

    def col_first(j):
        for xx in range(nx):
            ca_send[j, xx] = col_part[j, col_rows(xx * 2 + 1 - core), :].astype(BF16)
        send(ca_send.at[j], ca_recv.at[j], ca_s.at[j], ca_r.at[j], sib)

    def pair_sum(j, xx):
        return col_part[j, col_rows(xx * 2 + core), :] + ca_recv[j, xx].astype(F32)

    def col_second(j):
        arrived(ca_recv.at[j], ca_s.at[j], ca_r.at[j], sib)
        for k in range(1, nx):
            cb_send[j, k - 1] = pair_sum(j, lax.rem(x + k, nx)).astype(BF16)
            send(cb_send.at[j, k - 1], cb_recv.at[j, k - 1], cb_s.at[j, k - 1], cb_r.at[j, k - 1], x_dev(k))

    def col_last(j, out):
        value = pair_sum(j, x)
        for k in range(1, nx):
            arrived(cb_recv.at[j, k - 1], cb_s.at[j, k - 1], cb_r.at[j, k - 1], sib)
            value = value + cb_recv[j, k - 1].astype(F32)
        col_stage[j] = value.astype(BF16)
        copy = pltpu.make_async_copy(col_stage.at[j], out, out_sem.at[3 + j])
        copy.start()
        out_copies.append(copy)

    def transpose_hidden():
        def body(j, carry):
            c0 = al(j * BLK, BLK)
            hid_t[pl.ds(c0, BLK), :] = act[0, :, pl.ds(c0, BLK)].astype(F32).T.astype(BF16)
            return carry

        lax.fori_loop(0, fcb, body, 0)

    def down_dense():
        def body(j, carry):
            value = dot(hid_t[pl.ds(al(j * 2 * BLK, BLK), 2 * BLK), :], tcg[1])
            for a in range(2):
                for b in range(drb):
                    dense[(2 * j + a) * drb + b] = value[a * BLK : (a + 1) * BLK, b * BLK : (b + 1) * BLK]
            return carry

        lax.fori_loop(0, fcb // 2, body, 0)

    def wide_dense(t):
        def body(j, carry):
            value = dot(tok_t[...], act[t, :, pl.ds(al(j * 2 * BLK, BLK), 2 * BLK)])
            for a in range(drb):
                for b in range(2):
                    dense[a * fcb + 2 * j + b] = value[a * BLK : (a + 1) * BLK, b * BLK : (b + 1) * BLK]
            return carry

        lax.fori_loop(0, fcb // 2, body, 0)

    def layer_product():
        step = min(256, width)

        def body(j, carry):
            c0 = al(j * step, step)
            col_part[0, :, pl.ds(c0, step)] = dot(act[0], wd[:, pl.ds(c0, step)])
            return carry

        lax.fori_loop(0, width // step, body, 0)

    def grad_product(t, w):
        step = min(256, width)

        def body(j, carry):
            c0 = al(j * step, step)
            value = dot_t(act[t], w[pl.ds(c0, step), :])
            if t == 2:
                value = value + col_part[1, :, pl.ds(c0, step)]
            col_part[1, :, pl.ds(c0, step)] = value
            return carry

        lax.fori_loop(0, width // step, body, 0)

    stages = [[] for _ in range(steps + 5)]
    for t in range(3):
        for k in range(steps):
            stages[2 * t + k].append((t, k))
    for s in range(steps + 4):
        for t, k in stages[s]:
            ag_step(t, k)
        if s == steps:
            ag_step(0, steps)
            transpose_hidden()
            down_dense()
            emit_blocks(2)
            layer_product()
            col_first(0)
        if s == steps + 1:
            col_second(0)
        if s == steps + 2:
            ag_step(1, steps)
            wide_dense(1)
            emit_blocks(0)
            grad_product(1, wg)
        if s == steps + 3:
            col_last(0, layer_out)
    ag_step(2, steps)
    grad_product(2, wu)
    col_first(1)
    wide_dense(2)
    emit_blocks(1)
    col_second(1)
    finish_blocks(2, down_out)
    finish_blocks(0, gate_out)
    col_last(1, tgrad_out)
    finish_blocks(1, up_out)
    for c in out_copies:
        c.wait()
    for c in sends:
        c.wait_send()


def per_device(tokens, cotangent, gate_blocks, up_blocks, down_blocks, gate_slots, up_slots, down_slots):
    n_row, n_col = lax.axis_size("row"), lax.axis_size("col")
    n_tok, width = tokens.shape
    cap = gate_blocks.shape[2]
    hid = FF // n_col
    nz, nx = n_row // 2, n_col // 2
    steps = nz // 2
    group = n_tok * n_col
    zrows = group // nz
    own_rows = zrows // 2
    cw = hid // UNITS
    drb, fcb = width // BLK, hid // BLK
    hb = BLK // 2
    slots = jnp.concatenate([gate_slots[0], up_slots[0], down_slots[0]], axis=0)
    place = jnp.arange(drb * fcb, dtype=jnp.int32)
    order = jnp.arange(cap, dtype=jnp.int32)
    inv = jnp.min(
        jnp.where(slots[:, None, :] == place[None, :, None], order[None, None, :], cap), axis=2
    )
    slots = jnp.where(slots < 0, drb * fcb, slots)
    dims = (n_row, n_col, n_tok, width, hid, cap)
    smem = pl.BlockSpec(memory_space=pltpu.SMEM)
    anym = pl.BlockSpec(memory_space=pl.ANY)
    vm = pltpu.VMEM
    dma = pltpu.SemaphoreType.DMA
    scratch = [
        vm((3, cap + 1, BLK, BLK), BF16),
        vm((2, group, width), BF16),
        vm((width, hid), BF16),
        vm((width, hid), BF16),
        vm((hid, width), BF16),
        vm((3, group, hid), F32),
        vm((UNITS, 2, steps, 3, zrows, cw), BF16),
        vm((UNITS, 2, steps, 3, zrows, cw), BF16),
        vm((UNITS, 3, own_rows, cw), BF16),
        vm((UNITS, 3, own_rows, cw), BF16),
        vm((UNITS, 3, own_rows, cw), F32),
        vm((3, group, hid), BF16),
        vm((width, group), BF16),
        vm((hid, group), BF16),
        vm((drb * fcb + 1, BLK, BLK), F32),
        vm((3, cap, hb, BLK), BF16),
        vm((3, cap, hb, BLK), BF16),
        vm((3, cap, hb, BLK), F32),
        vm((2, group, width), F32),
        vm((2, nx, n_tok, width), BF16),
        vm((2, nx, n_tok, width), BF16),
        vm((2, nx - 1, n_tok, width), BF16),
        vm((2, nx - 1, n_tok, width), BF16),
        vm((2, n_tok, width), BF16),
        dma((5,)),
        dma((5,)),
        dma((2 * nx - 1,)),
        dma((2 * nx - 1,)),
        dma((UNITS, 2, steps)),
        dma((UNITS, 2, steps)),
        dma((UNITS,)),
        dma((UNITS,)),
        dma((UNITS,)),
        dma((UNITS,)),
        dma((3, UNITS, 2, steps)),
        dma((3, UNITS, 2, steps)),
        dma((3,)),
        dma((3,)),
        dma((2,)),
        dma((2,)),
        dma((2, nx - 1)),
        dma((2, nx - 1)),
    ]
    flops = 9 * 2 * group * width * hid
    layer, tgrad, gate_grad, up_grad, down_grad = pl.pallas_call(
        functools.partial(kernel, dims),
        out_shape=(
            jax.ShapeDtypeStruct((n_tok, width), BF16),
            jax.ShapeDtypeStruct((n_tok, width), BF16),
            jax.ShapeDtypeStruct((cap, hb, BLK), F32),
            jax.ShapeDtypeStruct((cap, hb, BLK), F32),
            jax.ShapeDtypeStruct((cap, hb, BLK), F32),
        ),
        in_specs=[smem, smem, anym, anym, anym, anym, anym],
        out_specs=(anym, anym, anym, anym, anym),
        scratch_shapes=scratch,
        compiler_params=pltpu.CompilerParams(
            collective_id=0, has_side_effects=True, vmem_limit_bytes=56 * 1024 * 1024
        ),
        cost_estimate=pl.CostEstimate(flops=flops, bytes_accessed=8 * 1024 * 1024, transcendentals=0),
        name="ffn",
    )(slots, inv, tokens, cotangent, gate_blocks[0, 0], up_blocks[0, 0], down_blocks[0, 0])
    return (layer, tgrad, gate_grad[None, None], up_grad[None, None], down_grad[None, None])


def solution(mesh):
    in_specs = (
        P(("col", "dp"), "row"),
        P(("col", "dp"), "row"),
        P("row", "col", None, None, None),
        P("row", "col", None, None, None),
        P("col", "row", None, None, None),
        P("row", "col", None),
        P("row", "col", None),
        P("col", "row", None),
    )
    out_specs = (
        P(("col", "dp"), "row"),
        P(("col", "dp"), "row"),
        P("row", "col", None, "dp", None),
        P("row", "col", None, "dp", None),
        P("col", "row", None, "dp", None),
    )
    return jax.shard_map(
        per_device, mesh=mesh, in_specs=in_specs, out_specs=out_specs, check_vma=False
    )
```

time: 1050 us -> 124 us (0.12)
  waiting for transfers between devices: 920 us -> 0 us
  Pallas kernels: 0 us -> 114 us
  matrix products: 50.4 us -> 0 us
  blocking collectives: 27.5 us -> 0 us
  local copies, waits for them, and re-layouts: 25.5 us -> 7.63 us
  between operations: 14.2 us -> 0.68 us
    reduce_scatter x8 -> x0, waiting for transfers between devices: 697 us -> none  [the longest x2 241 us: per_device(): lax.psum_scatter(block_apply(portion, down_tile, down_list, hidden_blocks...]
    all_gather x3 -> x0, waiting for transfers between devices: 221 us -> none  [the longest x1 76.9 us: per_device(): lax.all_gather(grad_up, 'row', axis=0, tiled=True)]
    pallas_call x0 -> x1, Pallas kernels: none -> 114 us  [per_device(): pl.pallas_call(functools.partial(kernel, dims), out_shape=(jax.ShapeDtype...]
    dot_general x27 -> x0, matrix products: 50.4 us -> none  [the longest x6 14.9 us: block_apply(): jnp.einsum(form, picked, blocks, preferred_element_type=jnp.float32)]
    all_gather x2 -> x0, blocking collectives: 27.5 us -> none  [the longest x1 14.1 us: per_device(): cotangent_full = lax.all_gather(cotangent, 'col', axis=0, tiled=True)]
    dot_general x3 -> x0, local copies, waits for them, and re-layouts: 11.7 us -> none  [block_apply(): picked = jnp.einsum('tnb,sn->stb', shaped, in_hot.astype(activations.dtype))]
  transfers between devices with their start and end apart: 11 -> 0, of which waited for: 10 -> 0; matrix products, arithmetic and copies ran while one was open for 6% -> 0% of each run, Pallas kernels for 0% -> 0%
where the time goes in v1:
time: 124 us
  Pallas kernels  114 us (92%)
  local copies, waits for them, and re-layouts  7.63 us (6%)
  other arithmetic  1.26 us (1%)
    pallas_call x1, Pallas kernels, per_device(): pl.pallas_call(functools.partial(kernel, dims), out_shape=(jax.ShapeDtype...  114 us
    unnamed x17, local copies, waits for them, and re-layouts  7.63 us

profile of v1, /device:TPU:8, one launch (start us, length us, event | category | flops | bytes accessed | tf_op | source)
XLA Modules:
  0.0 124.0 jit_solution(14504398233709528873)
XLA Ops:
  0.6 0.0 copy-start.3
  0.6 0.0 copy-start.4
  0.7 0.0 copy-start.5
  0.7 0.6 copy-done.3
  1.3 0.0 copy-done.4
  1.3 0.0 copy-done.5
  1.3 0.6 pad_add_fusion
  1.9 0.7 select_reduce_fusion.inv_ref
  2.6 114.4 %ffn.1 = (bf16[32,512]{1,0:T(8,128)(2,1)}, bf16[32,512]{1,0:T(8,128)(2,1)}, f32[32,64,128]{2,1,0:T(8,128)}, f32[32,64,128]{2,1,0:T(8,128)}, f32[32,64,128]{2,1,0:T(8,128)}) custom-call(s32[3,32]{1,0:T(4,128)} %get-tuple-element.16.slots_ref, s32[3,64]{1,0:T(4,128)} %select_reduce_fusion.inv_ref, bf16[32,512]{1,0:T(8,128)(2,1)} %tok_in.1, ...), custom_call_target="tpu_custom_call" | custom-call | flops 4831838208 | bytes 8388608 | tf_op jit(solution)/shard_map/ffn/pallas_call | solution.py:507
  117.0 0.0 copy-start.2
  117.0 1.4 %copy.18 = bf16[32,512]{1,0:T(8,128)(2,1)} copy(bf16[32,512]{1,0:T(8,128)(2,1)} %get-tuple-element.22) | data formatting | bytes 65536
  118.4 0.0 copy-done.2
  118.4 0.6 copy.19
  119.0 0.0 copy-start.1
  119.0 2.4 %copy.20 = f32[1,1,32,64,128]{4,3,2,1,0:T(8,128)} copy(f32[1,1,32,64,128]{4,3,2,1,0:T(8,128)} %bitcast.11) | data formatting | bytes 2097152
  121.4 0.0 copy-done.1
  121.4 0.0 copy-start
  121.4 1.0 copy.21
  122.4 0.6 copy-done
  123.0 1.0 copy.22
Async XLA Ops:
  0.6 0.7 copy-start.3
  0.6 0.7 copy-start.4
  0.7 0.7 copy-start.5
  117.0 1.4 %copy-start.2 = (bf16[32,512]{1,0:T(8,128)(2,1)S(1)}, bf16[32,512]{1,0:T(8,128)(2,1)}, u32[]{:S(2)}) copy-start(bf16[32,512]{1,0:T(8,128)(2,1)} %get-tuple-element.23) | copy-start | bytes 98308
  119.0 2.4 %copy-start.1 = (f32[32,64,128]{2,1,0:T(8,128)S(1)}, f32[32,64,128]{2,1,0:T(8,128)}, u32[]{:S(2)}) copy-start(f32[32,64,128]{2,1,0:T(8,128)} %get-tuple-element.13) | copy-start | bytes 3145732
  121.4 1.6 %copy-start = (f32[32,64,128]{2,1,0:T(8,128)S(1)}, f32[32,64,128]{2,1,0:T(8,128)}, u32[]{:S(2)}) copy-start(f32[32,64,128]{2,1,0:T(8,128)} %get-tuple-element.14) | copy-start | bytes 3145732

commit v2 on v1

v2 whole, which is shorter than its diff:
```python
import functools

import jax
import jax.numpy as jnp
from jax import lax
from jax.experimental import pallas as pl
from jax.experimental.pallas import tpu as pltpu
from jax.sharding import PartitionSpec as P

FF = 16384
BLK = 128
HB = BLK // 2
UNITS = 2
GRID = 4
MESH = pl.DeviceIdType.MESH
F32 = jnp.float32
BF16 = jnp.bfloat16


def dot(a, b):
    return lax.dot_general(a, b, (((1,), (0,)), ((), ())), preferred_element_type=F32)


def dot_t(a, b):
    return lax.dot_general(a, b, (((1,), (1,)), ((), ())), preferred_element_type=F32)


def al(value, step):
    return pl.multiple_of(value, step)


def swap(value):
    return pltpu.roll(value, HB, 1)


def lane_half(rows):
    return (lax.broadcasted_iota(jnp.int32, (rows, BLK), 1) >= HB).astype(jnp.int32)


def kernel(
    dims,
    slots_ref,
    inv_ref,
    tok_in,
    cot_in,
    gate_in,
    up_in,
    down_in,
    layer_out,
    tgrad_out,
    own_out,
    recv_out,
    down_out,
    blocks,
    tcg,
    wg,
    wu,
    wd,
    part,
    rs_send,
    rs_recv,
    y_send,
    y_recv,
    y_own,
    act,
    tok_t,
    hid_t,
    dense,
    dp_send,
    dp_own,
    down_own,
    col_part,
    ca_send,
    ca_recv,
    cb_send,
    cb_recv,
    cc_sum,
    cc_send,
    cc_recv,
    col_stage,
    loc_sem,
    out_sem,
    p1_s,
    p1_r,
    rs_s,
    rs_r,
    ys_s,
    ys_r,
    ya_s,
    ya_r,
    ag_s,
    ag_r,
    dp_s,
    dp_r,
    ca_s,
    ca_r,
    cb_s,
    cb_r,
    cc_s,
    cc_r,
):
    n_row, n_col, n_tok, width, hid, cap = dims
    nz, nx = n_row // 2, n_col // 2
    steps = nz // 2
    group = 2 * n_tok * n_col
    zrows = group // nz
    own_rows = zrows // 2
    cw = hid // UNITS
    half = cw // 2
    drb, fcb = width // BLK, hid // HB
    pair = 2 * n_tok

    row, col, dp = lax.axis_index("row"), lax.axis_index("col"), lax.axis_index("dp")
    z, yh = lax.div(row, 2), lax.rem(row, 2)
    x, core = lax.div(col, 2), lax.rem(col, 2)
    z_right = (lax.rem(z + 1, nz) * 2 + yh, col, dp)
    z_left = (lax.rem(z + nz - 1, nz) * 2 + yh, col, dp)
    z_dev = (z_right, z_left)
    y_dev = (z * 2 + 1 - yh, col, dp)
    sib = (row, x * 2 + 1 - core, dp)
    dp_dev = (row, col, 1 - dp)

    def x_dev(k):
        return (row, lax.rem(x + k, nx) * 2 + core, dp)

    sends = []

    def send(src, dst, s_sem, r_sem, dev):
        copy = pltpu.make_async_remote_copy(
            src_ref=src, dst_ref=dst, send_sem=s_sem, recv_sem=r_sem, device_id=dev, device_id_type=MESH
        )
        copy.start()
        sends.append(copy)

    def arrived(dst, s_sem, r_sem, dev):
        pltpu.make_async_remote_copy(
            src_ref=dst, dst_ref=dst, send_sem=s_sem, recv_sem=r_sem, device_id=dev, device_id_type=MESH
        ).wait_recv()

    mine = pl.ds(al((col * 2 + dp) * n_tok, n_tok), n_tok)
    own_loads = [
        pltpu.make_async_copy(ref, tcg.at[j, mine, :], loc_sem.at[j])
        for j, ref in enumerate((tok_in, cot_in))
    ]
    block_loads = [
        pltpu.make_async_copy(ref, blocks.at[i, pl.ds(0, cap)], loc_sem.at[2 + i])
        for i, ref in enumerate((gate_in, up_in, down_in))
    ]
    for c in own_loads + block_loads:
        c.start()

    barrier = pltpu.get_barrier_semaphore()
    peers = [z_right, z_left, y_dev, sib, dp_dev] + [x_dev(k) for k in range(1, nx)]
    for dev in peers:
        pl.semaphore_signal(barrier, inc=1, device_id=dev, device_id_type=MESH)
    pl.semaphore_wait(barrier, len(peers))

    def piece(j, xk, c, d):
        index = (lax.rem(x + nx - xk, nx) * 2 + c) * 2 + d
        return tcg.at[j, pl.ds(al(index * n_tok, n_tok), n_tok), :]

    def give(j, ref, s, dev):
        send(ref, ref, p1_s.at[j, s], p1_r.at[j, s], dev)

    def take(j, ref, s, dev):
        arrived(ref, p1_s.at[j, s], p1_r.at[j, s], dev)

    def gather_start(j):
        own_loads[j].wait()
        own = piece(j, 0, core, dp)
        for k in range(1, nx):
            give(j, own, k, x_dev(k))
        give(j, own, nx, dp_dev)
        give(j, own, 0, sib)

    def gather_x(j):
        for k in range(1, nx):
            ref = piece(j, k, core, dp)
            take(j, ref, k, sib)
            give(j, ref, nx + k, dp_dev)
            give(j, ref, 2 * nx + k - 1, sib)

    def gather_dp(j):
        for k in range(nx):
            ref = piece(j, k, core, 1 - dp)
            take(j, ref, nx + k, dp_dev)
            give(j, ref, 3 * nx - 1 + k, sib)

    def gather_sib(j):
        take(j, piece(j, 0, 1 - core, dp), 0, sib)
        for k in range(1, nx):
            take(j, piece(j, k, 1 - core, dp), 2 * nx + k - 1, sib)
        for k in range(nx):
            take(j, piece(j, k, 1 - core, 1 - dp), 3 * nx - 1 + k, sib)

    gather_start(0)
    gather_start(1)

    for c in block_loads:
        c.wait()
    for i in range(3):
        blocks[i, cap] = jnp.zeros((BLK, BLK), BF16)
    dense[drb * fcb] = jnp.zeros((BLK, BLK), F32)

    def place_wide(p, carry):
        r, c = p // (fcb // 2), p % (fcb // 2)
        keep = lane_half(BLK) == dp
        for i, w in enumerate((wg, wu)):
            even = blocks[i, inv_ref[i, 2 * p]].astype(F32)
            odd = blocks[i, inv_ref[i, 2 * p + 1]].astype(F32)
            stay = jnp.where(dp == 0, even, odd)
            move = swap(jnp.where(dp == 0, odd, even))
            w[pl.ds(al(r * BLK, BLK), BLK), pl.ds(al(c * BLK, BLK), BLK)] = jnp.where(
                keep, stay, move
            ).astype(BF16)
        return carry

    def place_down(p, carry):
        value = blocks[2, inv_ref[2, p]]
        r, c = p // drb, p % drb
        wd[pl.ds(al(r * HB, HB), HB), pl.ds(al(c * BLK, BLK), BLK)] = jnp.where(
            dp == 0, value[:HB], value[HB:]
        )
        return carry

    lax.fori_loop(0, drb * fcb // 2, place_wide, 0)
    gather_x(0)
    lax.fori_loop(0, drb * fcb, place_down, 0)
    gather_dp(0)
    gather_x(1)
    gather_sib(0)

    def z_rows(t):
        return al(lax.rem(t + 2 * nz, nz) * zrows, zrows)

    def rs_ref(buf, t, u, d, k):
        if k == 0:
            return buf.at[t, u, d, k, :, pl.ds(d * half, half)]
        return buf.at[t, u, d, k]

    def rs_start(t, u, d, k):
        target = z + (steps - k) * (1 - 2 * d)
        r0 = z_rows(target)
        for h in range(2):
            if k == 0 and h != d:
                continue
            hc = pl.ds(h * half, half)
            value = part[t, pl.ds(r0, zrows), pl.ds(u * cw + h * half, half)]
            if k > 1 or (k == 1 and h == d):
                value = value + rs_recv[t, u, d, k - 1, :, hc].astype(F32)
            rs_send[t, u, d, k, :, hc] = value.astype(BF16)
        send(
            rs_ref(rs_send, t, u, d, k),
            rs_ref(rs_recv, t, u, d, k),
            rs_s.at[t, u, d, k],
            rs_r.at[t, u, d, k],
            z_dev[d],
        )

    def rs_wait(t, u, d, k):
        arrived(rs_ref(rs_recv, t, u, d, k), rs_s.at[t, u, d, k], rs_r.at[t, u, d, k], z_dev[d])

    def rs_step(u, k):
        for t in range(3):
            for d in range(2):
                rs_wait(t, u, d, k - 1)
                rs_start(t, u, d, k)

    tile = min(256, cw)

    def product(t, u):
        def body(j, carry):
            cs = pl.ds(al(u * cw + j * tile, tile), tile)
            if t == 2:
                part[t, :, cs] = dot_t(tcg[1], wd[cs, :])
            else:
                part[t, :, cs] = dot(tcg[0], (wg, wu)[t][:, cs])
            return carry

        lax.fori_loop(0, cw // tile, body, 0)

    for t in range(2):
        product(t, 0)
        for d in range(2):
            rs_start(t, 0, d, 0)
    gather_dp(1)
    for t in range(2):
        product(t, 1)
    gather_sib(1)
    product(2, 0)
    for d in range(2):
        rs_start(2, 0, d, 0)

    mine_r = al(z * zrows + yh * own_rows, own_rows)
    theirs_r = al(z * zrows + (1 - yh) * own_rows, own_rows)
    mine_o, theirs_o = al(yh * own_rows, own_rows), al((1 - yh) * own_rows, own_rows)

    def rs_finish(u):
        for t in range(3):
            for d in range(2):
                rs_wait(t, u, d, steps - 1)

            def total(r0, o0):
                value = part[t, pl.ds(r0, own_rows), pl.ds(u * cw, cw)]
                for d in range(2):
                    value = value + rs_recv[t, u, d, steps - 1, pl.ds(o0, own_rows), :].astype(F32)
                return value

            y_send[u, t] = total(theirs_r, theirs_o).astype(BF16)
            y_own[u, t] = total(mine_r, mine_o)
        send(y_send.at[u], y_recv.at[u], ys_s.at[u], ys_r.at[u], y_dev)

    def act_rows(r0, u):
        return act.at[:, pl.ds(r0, own_rows), pl.ds(u * cw, cw)]

    def activate(u):
        arrived(y_recv.at[u], ys_s.at[u], ys_r.at[u], y_dev)
        for q in range(2):
            cs = pl.ds(q * half, half)
            gate = y_own[u, 0, :, cs] + y_recv[u, 0, :, cs].astype(F32)
            up = y_own[u, 1, :, cs] + y_recv[u, 1, :, cs].astype(F32)
            grad = y_own[u, 2, :, cs] + y_recv[u, 2, :, cs].astype(F32)
            sg = 1.0 / (1.0 + jnp.exp(-gate))
            co = pl.ds(u * cw + q * half, half)
            act[0, pl.ds(mine_r, own_rows), co] = (
                grad * up * sg * (1.0 + gate * (1.0 - sg))
            ).astype(BF16)
            act[1, pl.ds(mine_r, own_rows), co] = (grad * gate * sg).astype(BF16)
            act[2, pl.ds(mine_r, own_rows), co] = (gate * sg * up).astype(BF16)
        send(act_rows(mine_r, u), act_rows(mine_r, u), ya_s.at[u], ya_r.at[u], y_dev)

    def ag_slice(t, u, d, k, chunk):
        if k == steps - 1:
            c = pl.ds(u * cw + d * half, half)
        else:
            c = pl.ds(u * cw, cw)
        return act.at[t, pl.ds(z_rows(chunk), zrows), c]

    def ag_step(t, u, k):
        for d in range(2):
            sign = 1 - 2 * d
            if k > 0:
                ref = ag_slice(t, u, d, k - 1, z - k * sign)
                arrived(ref, ag_s.at[t, u, d, k - 1], ag_r.at[t, u, d, k - 1], z_dev[d])
            if k < steps:
                ref = ag_slice(t, u, d, k, z - k * sign)
                send(ref, ref, ag_s.at[t, u, d, k], ag_r.at[t, u, d, k], z_dev[d])

    out_copies = []

    def write_out(src, dst, index):
        copy = pltpu.make_async_copy(src, dst, out_sem.at[index])
        copy.start()
        out_copies.append(copy)

    def wide_dense(t):
        def body(j, carry):
            value = dot(tok_t[...], act[t, :, pl.ds(al(j * 2 * BLK, BLK), 2 * BLK)])
            low = lane_half(BLK) == 0
            for a in range(drb):
                for b in range(2):
                    both = value[a * BLK : (a + 1) * BLK, b * BLK : (b + 1) * BLK]
                    turned = swap(both)
                    dense[a * fcb + 4 * j + 2 * b] = jnp.where(low, both, turned)
                    dense[a * fcb + 4 * j + 2 * b + 1] = jnp.where(low, turned, both)
            return carry

        lax.fori_loop(0, fcb // 4, body, 0)

    def emit_wide(i):
        def body(s, carry):
            one = dense[slots_ref[i, s]]
            two = dense[slots_ref[i, s + cap // 2]]
            lanes = lane_half(HB)
            for h, value in enumerate((one, two)):
                keep = jnp.where(dp == 0, value[:HB], value[HB:])
                dp_own[i, h, s] = jnp.where(lanes == dp, keep, 0.0)
            give_one = jnp.where(dp == 0, one[HB:], one[:HB])
            give_two = jnp.where(dp == 0, two[HB:], two[:HB])
            dp_send[i, s] = jnp.where(lanes == 0, give_one, give_two).astype(BF16)
            return carry

        lax.fori_loop(0, cap // 2, body, 0)
        send(dp_send.at[i], recv_out.at[i], dp_s.at[i], dp_r.at[i], dp_dev)
        write_out(dp_own.at[i], own_out.at[i], i)

    def transpose_hidden(u):
        def body(j, carry):
            cs = pl.ds(al(u * cw + j * BLK, BLK), BLK)
            hid_t[cs, :] = act[2, :, cs].astype(F32).T.astype(BF16)
            return carry

        lax.fori_loop(0, cw // BLK, body, 0)

    def down_dense(u):
        per = cw // 256

        def body(j, carry):
            value = dot(hid_t[pl.ds(al(u * cw + j * 256, 256), 256), :], tcg[1])
            for a in range(4):
                for b in range(drb):
                    dense[(4 * (u * per + j) + a) * drb + b, pl.ds(0, HB)] = value[
                        a * HB : (a + 1) * HB, b * BLK : (b + 1) * BLK
                    ]
            return carry

        lax.fori_loop(0, per, body, 0)

    def emit_down():
        def body(s, carry):
            down_own[s] = dense[slots_ref[2, s], pl.ds(0, HB)]
            return carry

        lax.fori_loop(0, cap, body, 0)
        write_out(down_own, down_out, 2)

    def col_products(j, parts, first):
        step = min(256, width)

        def body(q, carry):
            cs = pl.ds(al(q * step, step), step)
            value = None if first else col_part[j, :, cs]
            for mul, a, b in parts:
                term = mul(a(), b(cs))
                value = term if value is None else value + term
            col_part[j, :, cs] = value
            return carry

        lax.fori_loop(0, width // step, body, 0)

    def layer_product(u):
        us = pl.ds(u * cw, cw)
        col_products(0, [(dot, lambda: act[2, :, us], lambda cs: wd[us, cs])], u == 0)

    def grad_product(t):
        w = (wg, wu)[t]
        col_products(1, [(dot_t, lambda: act[t], lambda cs: w[cs, :])], t == 0)

    def col_rows(c):
        return pl.ds(al(c * pair, pair), pair)

    def col_first(j):
        for xx in range(nx):
            ca_send[j, xx] = col_part[j, col_rows(xx * 2 + 1 - core), :].astype(BF16)
        send(ca_send.at[j], ca_recv.at[j], ca_s.at[j], ca_r.at[j], sib)

    def pair_sum(j, xx):
        return col_part[j, col_rows(xx * 2 + core), :] + ca_recv[j, xx].astype(F32)

    def col_second(j):
        arrived(ca_recv.at[j], ca_s.at[j], ca_r.at[j], sib)
        for k in range(1, nx):
            cb_send[j, k - 1] = pair_sum(j, lax.rem(x + k, nx)).astype(BF16)
            send(cb_send.at[j, k - 1], cb_recv.at[j, k - 1], cb_s.at[j, k - 1], cb_r.at[j, k - 1], x_dev(k))

    def col_third(j):
        value = pair_sum(j, x)
        for k in range(1, nx):
            arrived(cb_recv.at[j, k - 1], cb_s.at[j, k - 1], cb_r.at[j, k - 1], sib)
            value = value + cb_recv[j, k - 1].astype(F32)
        cc_sum[j] = value
        cc_send[j] = cc_sum[j, pl.ds(al((1 - dp) * n_tok, n_tok), n_tok), :].astype(BF16)
        send(cc_send.at[j], cc_recv.at[j], cc_s.at[j], cc_r.at[j], dp_dev)

    def col_last(j, out):
        arrived(cc_recv.at[j], cc_s.at[j], cc_r.at[j], dp_dev)
        value = cc_sum[j, pl.ds(al(dp * n_tok, n_tok), n_tok), :] + cc_recv[j].astype(F32)
        col_stage[j] = value.astype(BF16)
        write_out(col_stage.at[j], out, 3 + j)

    S = steps
    slots = {}

    def at(s, f, *a):
        slots.setdefault(s, []).append(functools.partial(f, *a))

    def y_arrived(u):
        arrived(act_rows(theirs_r, u), ya_s.at[u], ya_r.at[u], y_dev)

    def second_unit():
        product(2, 1)
        for t in range(3):
            for d in range(2):
                rs_start(t, 1, d, 0)

    def tok_transpose():
        tok_t[...] = tcg[0].astype(F32).T.astype(BF16)

    at(S, rs_finish, 0)
    at(S + 1, activate, 0)
    at(S + 2, y_arrived, 0)
    for k in range(1, S):
        at(k, rs_step, 0, k)
    at(S - 1, second_unit)
    for k in range(1, S):
        at(S - 1 + k, rs_step, 1, k)
    at(2 * S - 1, rs_finish, 1)
    at(2 * S, activate, 1)
    for k in range(S + 1):
        at(S + 2 + k, ag_step, 0, 0, k)
        at(S + 2 + k, ag_step, 1, 0, k)
        at(S + 3 + k, ag_step, 2, 0, k)
    at(2 * S + 1, y_arrived, 1)
    for k in range(S + 1):
        at(2 * S + 1 + k, ag_step, 0, 1, k)
        at(2 * S + 2 + k, ag_step, 1, 1, k)
        at(2 * S + 3 + k, ag_step, 2, 1, k)
    at(2 * S - 1, tok_transpose)
    at(2 * S + 4, transpose_hidden, 0)
    at(2 * S + 4, layer_product, 0)
    at(3 * S + 1, wide_dense, 0)
    at(3 * S + 1, emit_wide, 0)
    at(3 * S + 1, grad_product, 0)
    at(3 * S + 2, grad_product, 1)
    at(3 * S + 2, col_first, 1)
    at(3 * S + 2, wide_dense, 1)
    at(3 * S + 2, emit_wide, 1)
    at(3 * S + 2, col_second, 1)
    at(3 * S + 3, layer_product, 1)
    at(3 * S + 3, col_first, 0)
    at(3 * S + 3, col_third, 1)
    at(3 * S + 3, transpose_hidden, 1)
    at(3 * S + 3, col_second, 0)
    at(3 * S + 3, down_dense, 0)
    at(3 * S + 3, down_dense, 1)
    at(3 * S + 3, emit_down)
    at(3 * S + 3, col_third, 0)
    at(3 * S + 3, col_last, 1, tgrad_out)
    at(3 * S + 3, col_last, 0, layer_out)
    for s in sorted(slots):
        for f in slots[s]:
            f()
    for i in range(2):
        arrived(recv_out.at[i], dp_s.at[i], dp_r.at[i], dp_dev)
    for c in out_copies:
        c.wait()
    for c in sends:
        c.wait_send()


def finish(layer, tgrad, own, recv, down, layer_o, tgrad_o, gate_o, up_o, down_o):
    dp = lax.axis_index("dp")
    layer_o[...] = layer[...]
    tgrad_o[...] = tgrad[...]
    down_o[...] = down[...]
    lanes = lane_half(HB)
    for i, out in enumerate((gate_o, up_o)):
        for s in range(recv.shape[1]):
            value = recv[i, s].astype(F32)
            turned = swap(value)
            for h in range(2):
                other = jnp.where(dp == 1 - h, value, turned)
                out[h, s] = jnp.where(lanes == dp, own[i, h, s], other)


def per_device(tokens, cotangent, gate_blocks, up_blocks, down_blocks, gate_slots, up_slots, down_slots):
    n_row, n_col = lax.axis_size("row"), lax.axis_size("col")
    n_tok, width = tokens.shape
    cap = gate_blocks.shape[2]
    hid = FF // n_col // 2
    nz, nx = n_row // 2, n_col // 2
    steps = nz // 2
    group = 2 * n_tok * n_col
    zrows = group // nz
    own_rows = zrows // 2
    cw = hid // UNITS
    drb, fcb = width // BLK, hid // HB
    pair = 2 * n_tok
    slots = jnp.concatenate([gate_slots[0], up_slots[0], down_slots[0]], axis=0)
    place = jnp.arange(drb * fcb, dtype=jnp.int32)
    order = jnp.arange(cap, dtype=jnp.int32)
    inv = jnp.min(
        jnp.where(slots[:, None, :] == place[None, :, None], order[None, None, :], cap), axis=2
    )
    slots = jnp.where(slots < 0, drb * fcb, slots)
    dims = (n_row, n_col, n_tok, width, hid, cap)
    smem = pl.BlockSpec(memory_space=pltpu.SMEM)
    anym = pl.BlockSpec(memory_space=pl.ANY)
    vm = pltpu.VMEM
    dma = pltpu.SemaphoreType.DMA
    scratch = [
        vm((3, cap + 1, BLK, BLK), BF16),
        vm((2, group, width), BF16),
        vm((width, hid), BF16),
        vm((width, hid), BF16),
        vm((hid, width), BF16),
        vm((3, group, hid), F32),
        vm((3, UNITS, 2, steps, zrows, cw), BF16),
        vm((3, UNITS, 2, steps, zrows, cw), BF16),
        vm((UNITS, 3, own_rows, cw), BF16),
        vm((UNITS, 3, own_rows, cw), BF16),
        vm((UNITS, 3, own_rows, cw), F32),
        vm((3, group, hid), BF16),
        vm((width, group), BF16),
        vm((hid, group), BF16),
        vm((drb * fcb + 1, BLK, BLK), F32),
        vm((2, cap // 2, HB, BLK), BF16),
        vm((2, 2, cap // 2, HB, BLK), F32),
        vm((cap, HB, BLK), F32),
        vm((2, group, width), F32),
        vm((2, nx, pair, width), BF16),
        vm((2, nx, pair, width), BF16),
        vm((2, nx - 1, pair, width), BF16),
        vm((2, nx - 1, pair, width), BF16),
        vm((2, pair, width), F32),
        vm((2, n_tok, width), BF16),
        vm((2, n_tok, width), BF16),
        vm((2, n_tok, width), BF16),
        dma((5,)),
        dma((5,)),
        dma((2, 4 * nx - 1)),
        dma((2, 4 * nx - 1)),
        dma((3, UNITS, 2, steps)),
        dma((3, UNITS, 2, steps)),
        dma((UNITS,)),
        dma((UNITS,)),
        dma((UNITS,)),
        dma((UNITS,)),
        dma((3, UNITS, 2, steps)),
        dma((3, UNITS, 2, steps)),
        dma((2,)),
        dma((2,)),
        dma((2,)),
        dma((2,)),
        dma((2, nx - 1)),
        dma((2, nx - 1)),
        dma((2,)),
        dma((2,)),
    ]
    flops = 9 * 2 * group * width * hid
    inner = (
        jax.ShapeDtypeStruct((n_tok, width), BF16),
        jax.ShapeDtypeStruct((n_tok, width), BF16),
        jax.ShapeDtypeStruct((2, 2, cap // 2, HB, BLK), F32),
        jax.ShapeDtypeStruct((2, cap // 2, HB, BLK), BF16),
        jax.ShapeDtypeStruct((cap, HB, BLK), F32),
    )
    results = pl.pallas_call(
        functools.partial(kernel, dims),
        out_shape=inner,
        in_specs=[smem, smem, anym, anym, anym, anym, anym],
        out_specs=(anym,) * 5,
        scratch_shapes=scratch,
        compiler_params=pltpu.CompilerParams(
            collective_id=0, has_side_effects=True, vmem_limit_bytes=56 * 1024 * 1024
        ),
        cost_estimate=pl.CostEstimate(flops=flops, bytes_accessed=8 * 1024 * 1024, transcendentals=0),
        name="ffn",
    )(slots, inv, tokens, cotangent, gate_blocks[0, 0], up_blocks[0, 0], down_blocks[0, 0])
    ns = cap // 2 // GRID
    flat = pl.BlockSpec((n_tok, width), lambda g: (0, 0))
    wide = pl.BlockSpec((2, ns, HB, BLK), lambda g: (0, g, 0, 0))
    tall = pl.BlockSpec((2 * ns, HB, BLK), lambda g: (g, 0, 0))
    layer, tgrad, gate_grad, up_grad, down_grad = pl.pallas_call(
        finish,
        grid=(GRID,),
        out_shape=(
            inner[0],
            inner[1],
            jax.ShapeDtypeStruct((2, cap // 2, HB, BLK), F32),
            jax.ShapeDtypeStruct((2, cap // 2, HB, BLK), F32),
            inner[4],
        ),
        in_specs=[
            flat,
            flat,
            pl.BlockSpec((2, 2, ns, HB, BLK), lambda g: (0, 0, g, 0, 0)),
            wide,
            tall,
        ],
        out_specs=(flat, flat, wide, wide, tall),
        name="finish",
    )(*results)
    shape = (1, 1, cap, HB, BLK)
    return (layer, tgrad, gate_grad.reshape(shape), up_grad.reshape(shape), down_grad.reshape(shape))


def solution(mesh):
    in_specs = (
        P(("col", "dp"), "row"),
        P(("col", "dp"), "row"),
        P("row", "col", None, None, None),
        P("row", "col", None, None, None),
        P("col", "row", None, None, None),
        P("row", "col", None),
        P("row", "col", None),
        P("col", "row", None),
    )
    out_specs = (
        P(("col", "dp"), "row"),
        P(("col", "dp"), "row"),
        P("row", "col", None, "dp", None),
        P("row", "col", None, "dp", None),
        P("col", "row", None, "dp", None),
    )
    return jax.shard_map(
        per_device, mesh=mesh, in_specs=in_specs, out_specs=out_specs, check_vma=False
    )
```

time: 124 us -> 112 us (0.903)
  local copies, waits for them, and re-layouts: 7.63 us -> 0 us
  Pallas kernels: 114 us -> 110 us
    unnamed x17 -> x0, local copies, waits for them, and re-layouts: 7.63 us -> none
    pallas_call x1 -> x2, Pallas kernels: 114 us -> 110 us  [the longest x1 105 us: per_device(): pl.pallas_call(functools.partial(kernel, dims), out_shape=inner, in_specs...]
where the time goes in v2:
time: 112 us
  Pallas kernels  110 us (98%)
  other arithmetic  1.95 us (2%)
    pallas_call x1, Pallas kernels, per_device(): pl.pallas_call(functools.partial(kernel, dims), out_shape=inner, in_specs...  105 us
    pallas_call x1, Pallas kernels, per_device(): pl.pallas_call(finish, grid=(GRID,), out_shape=(inner[0], inner[1], jax.S...  4.37 us

profile of v2, /device:TPU:8, one launch (start us, length us, event | category | flops | bytes accessed | tf_op | source)
XLA Modules:
  0.0 112.2 jit_solution(11104477904392204194)
XLA Ops:
  0.6 1.3 %pad_add_fusion = (s32[3,32]{1,0:T(4,128)S(1)}, s32[3,32]{1,0:T(4,128)}) fusion(s32[1,32]{1,0:T(1,128)} %bitcast.9, s32[1,32]{1,0:T(1,128)} %bitcast.10, s32[1,32]{1,0:T(1,128)} %bitcast.11), kind=kLoop, calls=%fused_computation.3 | loop fusion | flops 384 | bytes 1152 | tf_op jit(solution)/shard_map/concatenate | solution.py:569
  1.9 0.7 select_reduce_fusion.inv_ref
  2.6 105.3 %ffn.1 = (bf16[32,512]{1,0:T(8,128)(2,1)}, bf16[32,512]{1,0:T(8,128)(2,1)}, f32[2,2,16,64,128]{4,3,2,1,0:T(8,128)}, bf16[2,16,64,128]{3,2,1,0:T(8,128)(2,1)}, f32[32,64,128]{2,1,0:T(8,128)}) custom-call(s32[3,32]{1,0:T(4,128)} %get-tuple-element.26.slots_ref, s32[3,64]{1,0:T(4,128)} %select_reduce_fusion.inv_ref, bf16[32,512]{1,0:T(8,128)(2,1)} %tok_in.1, ...), custom_call_target="tpu_custom_call" | custom-call | flops 4831838208 | bytes 8388608 | tf_op jit(solution)/shard_map/ffn/pallas_call | solution.py:638
  107.9 4.4 %finish.1 = (bf16[32,512]{1,0:T(8,128)(2,1)}, bf16[32,512]{1,0:T(8,128)(2,1)}, f32[2,16,64,128]{3,2,1,0:T(8,128)}, f32[2,16,64,128]{3,2,1,0:T(8,128)}, f32[32,64,128]{2,1,0:T(8,128)}) custom-call(bf16[32,512]{1,0:T(8,128)(2,1)} %get-tuple-element.15.layer, bf16[32,512]{1,0:T(8,128)(2,1)} %get-tuple-element.16.tgrad, ...), custom_call_target="tpu_custom_call" | custom-call | tf_op jit(solution)/shard_map/finish/pallas_call | solution.py:654

commit v3 on v2

--- a/solution.py
+++ b/solution.py
@@ -62,10 +62,14 @@
     y_send,
     y_recv,
     y_own,
+    yb_send,
+    yb_recv,
     act,
     tok_t,
     hid_t,
-    dense,
+    dense_g,
+    dense_u,
+    dense_d,
     dp_send,
     dp_own,
     down_own,
@@ -86,8 +90,14 @@
     rs_r,
     ys_s,
     ys_r,
+    yb_s,
+    yb_r,
     ya_s,
     ya_r,
+    az_s,
+    az_r,
+    ay_s,
+    ay_r,
     ag_s,
     ag_r,
     dp_s,
@@ -120,8 +130,8 @@
     sib = (row, x * 2 + 1 - core, dp)
     dp_dev = (row, col, 1 - dp)
 
-    def x_dev(k):
-        return (row, lax.rem(x + k, nx) * 2 + core, dp)
+    def x_dev(k, d):
+        return (row, lax.rem(x + k, nx) * 2 + core, d)
 
     sends = []
 
@@ -150,48 +160,43 @@
         c.start()
 
     barrier = pltpu.get_barrier_semaphore()
-    peers = [z_right, z_left, y_dev, sib, dp_dev] + [x_dev(k) for k in range(1, nx)]
+    peers = [z_right, z_left, y_dev, sib, dp_dev] + [
+        x_dev(k, d) for k in range(1, nx) for d in (dp, 1 - dp)
+    ]
     for dev in peers:
         pl.semaphore_signal(barrier, inc=1, device_id=dev, device_id_type=MESH)
     pl.semaphore_wait(barrier, len(peers))
 
-    def piece(j, xk, c, d):
-        index = (lax.rem(x + nx - xk, nx) * 2 + c) * 2 + d
-        return tcg.at[j, pl.ds(al(index * n_tok, n_tok), n_tok), :]
+    def rows_of(j, index, n):
+        return tcg.at[j, pl.ds(al(index * n_tok, n_tok), n * n_tok), :]
+
+    def source(k, c):
+        return (lax.rem(x + nx - k, nx) * 2 + c) * 2
 
     def give(j, ref, s, dev):
         send(ref, ref, p1_s.at[j, s], p1_r.at[j, s], dev)
 
-    def take(j, ref, s, dev):
-        arrived(ref, p1_s.at[j, s], p1_r.at[j, s], dev)
+    def take(j, ref, s):
+        arrived(ref, p1_s.at[j, s], p1_r.at[j, s], sib)
 
     def gather_start(j):
         own_loads[j].wait()
-        own = piece(j, 0, core, dp)
+        own = rows_of(j, source(0, core) + dp, 1)
         for k in range(1, nx):
-            give(j, own, k, x_dev(k))
+            give(j, own, k, x_dev(k, dp))
+            give(j, own, nx + k, x_dev(k, 1 - dp))
         give(j, own, nx, dp_dev)
-        give(j, own, 0, sib)
-
-    def gather_x(j):
-        for k in range(1, nx):
-            ref = piece(j, k, core, dp)
-            take(j, ref, k, sib)
-            give(j, ref, nx + k, dp_dev)
-            give(j, ref, 2 * nx + k - 1, sib)
-
-    def gather_dp(j):
+
+    def gather_pass(j):
         for k in range(nx):
-            ref = piece(j, k, core, 1 - dp)
-            take(j, ref, nx + k, dp_dev)
-            give(j, ref, 3 * nx - 1 + k, sib)
-
-    def gather_sib(j):
-        take(j, piece(j, 0, 1 - core, dp), 0, sib)
-        for k in range(1, nx):
-            take(j, piece(j, k, 1 - core, dp), 2 * nx + k - 1, sib)
+            if k > 0:
+                take(j, rows_of(j, source(k, core) + dp, 1), k)
+            take(j, rows_of(j, source(k, core) + 1 - dp, 1), nx + k)
+            give(j, rows_of(j, source(k, core), 2), 2 * nx + k - 1 if k else 0, sib)
+
+    def gather_end(j):
         for k in range(nx):
-            take(j, piece(j, k, 1 - core, 1 - dp), 3 * nx - 1 + k, sib)
+            take(j, rows_of(j, source(k, 1 - core), 2), 2 * nx + k - 1 if k else 0)
 
     gather_start(0)
     gather_start(1)
@@ -200,7 +205,8 @@
         c.wait()
     for i in range(3):
         blocks[i, cap] = jnp.zeros((BLK, BLK), BF16)
-    dense[drb * fcb] = jnp.zeros((BLK, BLK), F32)
+    for ref in (dense_g, dense_u, dense_d):
+        ref[drb * fcb] = jnp.zeros(ref.shape[1:], F32)
 
     def place_wide(p, carry):
         r, c = p // (fcb // 2), p % (fcb // 2)
@@ -224,31 +230,36 @@
         return carry
 
     lax.fori_loop(0, drb * fcb // 2, place_wide, 0)
-    gather_x(0)
     lax.fori_loop(0, drb * fcb, place_down, 0)
-    gather_dp(0)
-    gather_x(1)
-    gather_sib(0)
+    gather_pass(0)
+    gather_end(0)
 
     def z_rows(t):
         return al(lax.rem(t + 2 * nz, nz) * zrows, zrows)
 
+    def unit_rows(u, target):
+        if u == 0:
+            return z_rows(target)
+        return al(z_rows(target) + yh * own_rows, own_rows)
+
+    count = (zrows, own_rows)
+
     def rs_ref(buf, t, u, d, k):
-        if k == 0:
-            return buf.at[t, u, d, k, :, pl.ds(d * half, half)]
-        return buf.at[t, u, d, k]
+        cs = pl.ds(d * half, half) if k == 0 else pl.ds(0, cw)
+        return buf.at[t, u, d, k, pl.ds(0, count[u]), cs]
 
     def rs_start(t, u, d, k):
         target = z + (steps - k) * (1 - 2 * d)
-        r0 = z_rows(target)
+        rs = pl.ds(unit_rows(u, target), count[u])
+        to = pl.ds(0, count[u])
         for h in range(2):
             if k == 0 and h != d:
                 continue
             hc = pl.ds(h * half, half)
-            value = part[t, pl.ds(r0, zrows), pl.ds(u * cw + h * half, half)]
+            value = part[t, rs, pl.ds(u * cw + h * half, half)]
             if k > 1 or (k == 1 and h == d):
-                value = value + rs_recv[t, u, d, k - 1, :, hc].astype(F32)
-            rs_send[t, u, d, k, :, hc] = value.astype(BF16)
+                value = value + rs_recv[t, u, d, k - 1, to, hc].astype(F32)
+            rs_send[t, u, d, k, to, hc] = value.astype(BF16)
         send(
             rs_ref(rs_send, t, u, d, k),
             rs_ref(rs_recv, t, u, d, k),
@@ -260,11 +271,24 @@
     def rs_wait(t, u, d, k):
         arrived(rs_ref(rs_recv, t, u, d, k), rs_s.at[t, u, d, k], rs_r.at[t, u, d, k], z_dev[d])
 
-    def rs_step(u, k):
-        for t in range(3):
-            for d in range(2):
-                rs_wait(t, u, d, k - 1)
-                rs_start(t, u, d, k)
+    def rs_step(t, u, k):
+        for d in range(2):
+            rs_wait(t, u, d, k - 1)
+            rs_start(t, u, d, k)
+
+    def yb_start(t):
+        for c in range(nz):
+            r0 = al(c * zrows + (1 - yh) * own_rows, own_rows)
+            yb_send[t, c] = part[t, pl.ds(r0, own_rows), pl.ds(cw, cw)].astype(BF16)
+        send(yb_send.at[t], yb_recv.at[t], yb_s.at[t], yb_r.at[t], y_dev)
+
+    def yb_add(t):
+        arrived(yb_recv.at[t], yb_s.at[t], yb_r.at[t], y_dev)
+        for c in range(nz):
+            rs = pl.ds(al(c * zrows + yh * own_rows, own_rows), own_rows)
+            part[t, rs, pl.ds(cw, cw)] = part[t, rs, pl.ds(cw, cw)] + yb_recv[t, c].astype(F32)
+        for d in range(2):
+            rs_start(t, 1, d, 0)
 
     tile = min(256, cw)
 
@@ -283,43 +307,51 @@
         product(t, 0)
         for d in range(2):
             rs_start(t, 0, d, 0)
-    gather_dp(1)
-    for t in range(2):
         product(t, 1)
-    gather_sib(1)
+        yb_start(t)
+        if t == 0:
+            gather_pass(1)
+    gather_end(1)
     product(2, 0)
     for d in range(2):
         rs_start(2, 0, d, 0)
+    product(2, 1)
+    yb_start(2)
 
     mine_r = al(z * zrows + yh * own_rows, own_rows)
     theirs_r = al(z * zrows + (1 - yh) * own_rows, own_rows)
     mine_o, theirs_o = al(yh * own_rows, own_rows), al((1 - yh) * own_rows, own_rows)
 
-    def rs_finish(u):
-        for t in range(3):
-            for d in range(2):
-                rs_wait(t, u, d, steps - 1)
-
-            def total(r0, o0):
-                value = part[t, pl.ds(r0, own_rows), pl.ds(u * cw, cw)]
-                for d in range(2):
-                    value = value + rs_recv[t, u, d, steps - 1, pl.ds(o0, own_rows), :].astype(F32)
-                return value
-
-            y_send[u, t] = total(theirs_r, theirs_o).astype(BF16)
-            y_own[u, t] = total(mine_r, mine_o)
-        send(y_send.at[u], y_recv.at[u], ys_s.at[u], ys_r.at[u], y_dev)
-
-    def act_rows(r0, u):
+    def last_sum(t, u, r0, o0):
+        value = part[t, pl.ds(r0, own_rows), pl.ds(u * cw, cw)]
+        for d in range(2):
+            value = value + rs_recv[t, u, d, steps - 1, pl.ds(o0, own_rows), :].astype(F32)
+        return value
+
+    def rs_finish(t, u):
+        for d in range(2):
+            rs_wait(t, u, d, steps - 1)
+        if u == 0:
+            y_send[t] = last_sum(t, u, theirs_r, theirs_o).astype(BF16)
+            y_own[u, t] = last_sum(t, u, mine_r, mine_o)
+            if t == 2:
+                send(y_send, y_recv, ys_s.at[0], ys_r.at[0], y_dev)
+        else:
+            y_own[u, t] = last_sum(t, u, mine_r, 0)
+
+    def rows_ref(r0, u):
         return act.at[:, pl.ds(r0, own_rows), pl.ds(u * cw, cw)]
 
     def activate(u):
-        arrived(y_recv.at[u], ys_s.at[u], ys_r.at[u], y_dev)
+        if u == 0:
+            arrived(y_recv, ys_s.at[0], ys_r.at[0], y_dev)
         for q in range(2):
             cs = pl.ds(q * half, half)
-            gate = y_own[u, 0, :, cs] + y_recv[u, 0, :, cs].astype(F32)
-            up = y_own[u, 1, :, cs] + y_recv[u, 1, :, cs].astype(F32)
-            grad = y_own[u, 2, :, cs] + y_recv[u, 2, :, cs].astype(F32)
+            gate, up, grad = (y_own[u, t, :, cs] for t in range(3))
+            if u == 0:
+                gate = gate + y_recv[0, :, cs].astype(F32)
+                up = up + y_recv[1, :, cs].astype(F32)
+                grad = grad + y_recv[2, :, cs].astype(F32)
             sg = 1.0 / (1.0 + jnp.exp(-gate))
             co = pl.ds(u * cw + q * half, half)
             act[0, pl.ds(mine_r, own_rows), co] = (
@@ -327,24 +359,51 @@
             ).astype(BF16)
             act[1, pl.ds(mine_r, own_rows), co] = (grad * gate * sg).astype(BF16)
             act[2, pl.ds(mine_r, own_rows), co] = (gate * sg * up).astype(BF16)
-        send(act_rows(mine_r, u), act_rows(mine_r, u), ya_s.at[u], ya_r.at[u], y_dev)
-
-    def ag_slice(t, u, d, k, chunk):
+        ref = rows_ref(mine_r, u)
+        if u == 0:
+            send(ref, ref, ay_s.at[0, steps], ay_r.at[0, steps], y_dev)
+        else:
+            send(ref, ref, ya_s.at[0], ya_r.at[0], y_dev)
+
+    def az_chunk(d, k, hops, hi):
+        rs = pl.ds(al(z_rows(z - hops * (1 - 2 * d)) + hi * own_rows, own_rows), own_rows)
+        cs = pl.ds(d * half, half) if k == steps - 1 else pl.ds(0, cw)
+        return act.at[:, rs, cs]
+
+    def az_step(k):
+        for d in range(2):
+            if k > 0:
+                ref = az_chunk(d, k - 1, k, yh)
+                arrived(ref, az_s.at[d, k - 1], az_r.at[d, k - 1], z_dev[d])
+            if k < steps:
+                out = az_chunk(d, k, k, yh)
+                send(out, out, az_s.at[d, k], az_r.at[d, k], z_dev[d])
+            if k > 0:
+                send(ref, ref, ay_s.at[d, k - 1], ay_r.at[d, k - 1], y_dev)
+
+    def ay_wait():
+        arrived(rows_ref(theirs_r, 0), ay_s.at[0, steps], ay_r.at[0, steps], y_dev)
+        for k in range(1, steps + 1):
+            for d in range(2):
+                ref = az_chunk(d, k - 1, k, 1 - yh)
+                arrived(ref, ay_s.at[d, k - 1], ay_r.at[d, k - 1], y_dev)
+
+    def ag_slice(t, d, k, chunk):
         if k == steps - 1:
-            c = pl.ds(u * cw + d * half, half)
+            c = pl.ds(cw + d * half, half)
         else:
-            c = pl.ds(u * cw, cw)
+            c = pl.ds(cw, cw)
         return act.at[t, pl.ds(z_rows(chunk), zrows), c]
 
-    def ag_step(t, u, k):
+    def ag_step(t, k):
         for d in range(2):
             sign = 1 - 2 * d
             if k > 0:
-                ref = ag_slice(t, u, d, k - 1, z - k * sign)
-                arrived(ref, ag_s.at[t, u, d, k - 1], ag_r.at[t, u, d, k - 1], z_dev[d])
+                ref = ag_slice(t, d, k - 1, z - k * sign)
+                arrived(ref, ag_s.at[t, d, k - 1], ag_r.at[t, d, k - 1], z_dev[d])
             if k < steps:
-                ref = ag_slice(t, u, d, k, z - k * sign)
-                send(ref, ref, ag_s.at[t, u, d, k], ag_r.at[t, u, d, k], z_dev[d])
+                ref = ag_slice(t, d, k, z - k * sign)
+                send(ref, ref, ag_s.at[t, d, k], ag_r.at[t, d, k], z_dev[d])
 
     out_copies = []
 
@@ -353,21 +412,27 @@
         copy.start()
         out_copies.append(copy)
 
-    def wide_dense(t):
+    def wide_dense(t, u):
+        dense = (dense_g, dense_u)[t]
+        per = cw // (2 * BLK)
+
         def body(j, carry):
-            value = dot(tok_t[...], act[t, :, pl.ds(al(j * 2 * BLK, BLK), 2 * BLK)])
+            value = dot(tok_t[...], act[t, :, pl.ds(al(u * cw + j * 2 * BLK, BLK), 2 * BLK)])
             low = lane_half(BLK) == 0
             for a in range(drb):
                 for b in range(2):
                     both = value[a * BLK : (a + 1) * BLK, b * BLK : (b + 1) * BLK]
                     turned = swap(both)
-                    dense[a * fcb + 4 * j + 2 * b] = jnp.where(low, both, turned)
-                    dense[a * fcb + 4 * j + 2 * b + 1] = jnp.where(low, turned, both)
+                    c = 4 * (u * per + j) + 2 * b
+                    dense[a * fcb + c] = jnp.where(low, both, turned)
+                    dense[a * fcb + c + 1] = jnp.where(low, turned, both)
             return carry
 
-        lax.fori_loop(0, fcb // 4, body, 0)
+        lax.fori_loop(0, per, body, 0)
 
     def emit_wide(i):
+        dense = (dense_g, dense_u)[i]
+
         def body(s, carry):
             one = dense[slots_ref[i, s]]
             two = dense[slots_ref[i, s + cap // 2]]
@@ -399,7 +464,7 @@
             value = dot(hid_t[pl.ds(al(u * cw + j * 256, 256), 256), :], tcg[1])
             for a in range(4):
                 for b in range(drb):
-                    dense[(4 * (u * per + j) + a) * drb + b, pl.ds(0, HB)] = value[
+                    dense_d[(4 * (u * per + j) + a) * drb + b] = value[
                         a * HB : (a + 1) * HB, b * BLK : (b + 1) * BLK
                     ]
             return carry
@@ -408,7 +473,7 @@
 
     def emit_down():
         def body(s, carry):
-            down_own[s] = dense[slots_ref[2, s], pl.ds(0, HB)]
+            down_own[s] = dense_d[slots_ref[2, s]]
             return carry
 
         lax.fori_loop(0, cap, body, 0)
@@ -432,9 +497,13 @@
         us = pl.ds(u * cw, cw)
         col_products(0, [(dot, lambda: act[2, :, us], lambda cs: wd[us, cs])], u == 0)
 
-    def grad_product(t):
-        w = (wg, wu)[t]
-        col_products(1, [(dot_t, lambda: act[t], lambda cs: w[cs, :])], t == 0)
+    def grad_product(u):
+        us = pl.ds(u * cw, cw)
+        parts = [
+            (dot_t, lambda: act[0, :, us], lambda cs: wg[cs, us]),
+            (dot_t, lambda: act[1, :, us], lambda cs: wu[cs, us]),
+        ]
+        col_products(1, parts, u == 0)
 
     def col_rows(c):
         return pl.ds(al(c * pair, pair), pair)
@@ -451,7 +520,7 @@
         arrived(ca_recv.at[j], ca_s.at[j], ca_r.at[j], sib)
         for k in range(1, nx):
             cb_send[j, k - 1] = pair_sum(j, lax.rem(x + k, nx)).astype(BF16)
-            send(cb_send.at[j, k - 1], cb_recv.at[j, k - 1], cb_s.at[j, k - 1], cb_r.at[j, k - 1], x_dev(k))
+            send(cb_send.at[j, k - 1], cb_recv.at[j, k - 1], cb_s.at[j, k - 1], cb_r.at[j, k - 1], x_dev(k, dp))
 
     def col_third(j):
         value = pair_sum(j, x)
@@ -474,59 +543,66 @@
     def at(s, f, *a):
         slots.setdefault(s, []).append(functools.partial(f, *a))
 
-    def y_arrived(u):
-        arrived(act_rows(theirs_r, u), ya_s.at[u], ya_r.at[u], y_dev)
-
-    def second_unit():
-        product(2, 1)
-        for t in range(3):
-            for d in range(2):
-                rs_start(t, 1, d, 0)
+    def y_arrived():
+        arrived(rows_ref(theirs_r, 1), ya_s.at[0], ya_r.at[0], y_dev)
 
     def tok_transpose():
         tok_t[...] = tcg[0].astype(F32).T.astype(BF16)
 
-    at(S, rs_finish, 0)
+    for k in range(1, S):
+        for t in range(3):
+            at(k, rs_step, t, 0, k)
+    at(S - 1, yb_add, 0)
+    at(S - 1, yb_add, 1)
+    for t in range(3):
+        at(S, rs_finish, t, 0)
+    at(S, rs_step, 0, 1, 1)
+    at(S, rs_step, 1, 1, 1)
+    at(S, yb_add, 2)
     at(S + 1, activate, 0)
-    at(S + 2, y_arrived, 0)
+    for k in range(S + 1):
+        at(S + 1 + k, az_step, k)
+    for k in range(2, S):
+        at(S - 1 + k, rs_step, 0, 1, k)
+        at(S - 1 + k, rs_step, 1, 1, k)
     for k in range(1, S):
-        at(k, rs_step, 0, k)
-    at(S - 1, second_unit)
-    for k in range(1, S):
-        at(S - 1 + k, rs_step, 1, k)
-    at(2 * S - 1, rs_finish, 1)
+        at(S + k, rs_step, 2, 1, k)
+    at(2 * S - 1, tok_transpose)
+    for t in range(3):
+        at(2 * S, rs_finish, t, 1)
     at(2 * S, activate, 1)
+    at(2 * S + 1, y_arrived)
     for k in range(S + 1):
-        at(S + 2 + k, ag_step, 0, 0, k)
-        at(S + 2 + k, ag_step, 1, 0, k)
-        at(S + 3 + k, ag_step, 2, 0, k)
-    at(2 * S + 1, y_arrived, 1)
-    for k in range(S + 1):
-        at(2 * S + 1 + k, ag_step, 0, 1, k)
-        at(2 * S + 2 + k, ag_step, 1, 1, k)
-        at(2 * S + 3 + k, ag_step, 2, 1, k)
-    at(2 * S - 1, tok_transpose)
-    at(2 * S + 4, transpose_hidden, 0)
-    at(2 * S + 4, layer_product, 0)
-    at(3 * S + 1, wide_dense, 0)
-    at(3 * S + 1, emit_wide, 0)
-    at(3 * S + 1, grad_product, 0)
-    at(3 * S + 2, grad_product, 1)
-    at(3 * S + 2, col_first, 1)
-    at(3 * S + 2, wide_dense, 1)
-    at(3 * S + 2, emit_wide, 1)
-    at(3 * S + 2, col_second, 1)
-    at(3 * S + 3, layer_product, 1)
-    at(3 * S + 3, col_first, 0)
-    at(3 * S + 3, col_third, 1)
-    at(3 * S + 3, transpose_hidden, 1)
-    at(3 * S + 3, col_second, 0)
-    at(3 * S + 3, down_dense, 0)
-    at(3 * S + 3, down_dense, 1)
-    at(3 * S + 3, emit_down)
-    at(3 * S + 3, col_third, 0)
-    at(3 * S + 3, col_last, 1, tgrad_out)
-    at(3 * S + 3, col_last, 0, layer_out)
+        at(2 * S + 1 + k, ag_step, 0, k)
+        at(2 * S + 1 + k, ag_step, 1, k)
+        at(2 * S + 2 + k, ag_step, 2, k)
+    A = 3 * S
+    at(A, ay_wait)
+    at(A, wide_dense, 0, 0)
+    at(A, wide_dense, 1, 0)
+    at(A, grad_product, 0)
+    A = 3 * S + 1
+    at(A, wide_dense, 0, 1)
+    at(A, emit_wide, 0)
+    at(A, grad_product, 1)
+    at(A, col_first, 1)
+    at(A, wide_dense, 1, 1)
+    at(A, emit_wide, 1)
+    at(A, col_second, 1)
+    at(A, layer_product, 0)
+    at(A, transpose_hidden, 0)
+    at(A, down_dense, 0)
+    at(A, col_third, 1)
+    A = 3 * S + 2
+    at(A, layer_product, 1)
+    at(A, col_first, 0)
+    at(A, transpose_hidden, 1)
+    at(A, col_second, 0)
+    at(A, down_dense, 1)
+    at(A, emit_down)
+    at(A, col_third, 0)
+    at(A, col_last, 1, tgrad_out)
+    at(A, col_last, 0, layer_out)
     for s in sorted(slots):
         for f in slots[s]:
             f()
@@ -587,13 +663,17 @@
         vm((3, group, hid), F32),
         vm((3, UNITS, 2, steps, zrows, cw), BF16),
         vm((3, UNITS, 2, steps, zrows, cw), BF16),
-        vm((UNITS, 3, own_rows, cw), BF16),
-        vm((UNITS, 3, own_rows, cw), BF16),
+        vm((3, own_rows, cw), BF16),
+        vm((3, own_rows, cw), BF16),
         vm((UNITS, 3, own_rows, cw), F32),
+        vm((3, nz, own_rows, cw), BF16),
+        vm((3, nz, own_rows, cw), BF16),
         vm((3, group, hid), BF16),
         vm((width, group), BF16),
         vm((hid, group), BF16),
         vm((drb * fcb + 1, BLK, BLK), F32),
+        vm((drb * fcb + 1, BLK, BLK), F32),
+        vm((drb * fcb + 1, HB, BLK), F32),
         vm((2, cap // 2, HB, BLK), BF16),
         vm((2, 2, cap // 2, HB, BLK), F32),
         vm((cap, HB, BLK), F32),
@@ -608,16 +688,22 @@
         vm((2, n_tok, width), BF16),
         dma((5,)),
         dma((5,)),
-        dma((2, 4 * nx - 1)),
-        dma((2, 4 * nx - 1)),
+        dma((2, 3 * nx - 1)),
+        dma((2, 3 * nx - 1)),
         dma((3, UNITS, 2, steps)),
         dma((3, UNITS, 2, steps)),
-        dma((UNITS,)),
-        dma((UNITS,)),
-        dma((UNITS,)),
-        dma((UNITS,)),
-        dma((3, UNITS, 2, steps)),
-        dma((3, UNITS, 2, steps)),
+        dma((1,)),
+        dma((1,)),
+        dma((3,)),
+        dma((3,)),
+        dma((1,)),
+        dma((1,)),
+        dma((2, steps)),
+        dma((2, steps)),
+        dma((2, steps + 1)),
+        dma((2, steps + 1)),
+        dma((3, 2, steps)),
+        dma((3, 2, steps)),
         dma((2,)),
         dma((2,)),
         dma((2,)),

time: 112 us -> 109 us (0.973)
  Pallas kernels: 110 us -> 106 us
    pallas_call x1, Pallas kernels: 105 us -> 101 us  [per_device(): pl.pallas_call(functools.partial(kernel, dims), out_shape=inner, in_specs...]
where the time goes in v3:
time: 109 us; the launch traced here: 108 us
  Pallas kernels  106 us (97%)
  other arithmetic  1.95 us (2%)
    pallas_call x1, Pallas kernels, per_device(): pl.pallas_call(functools.partial(kernel, dims), out_shape=inner, in_specs...  101 us
    pallas_call x1, Pallas kernels, per_device(): pl.pallas_call(finish, grid=(GRID,), out_shape=(inner[0], inner[1], jax.S...  4.37 us

profile of v3, /device:TPU:8, one launch (start us, length us, event | category | flops | bytes accessed | tf_op | source)
XLA Modules:
  0.0 108.2 jit_solution(10505202563475443683)
XLA Ops:
  0.6 1.3 %pad_add_fusion = (s32[3,32]{1,0:T(4,128)S(1)}, s32[3,32]{1,0:T(4,128)}) fusion(s32[1,32]{1,0:T(1,128)} %bitcast.9, s32[1,32]{1,0:T(1,128)} %bitcast.10, s32[1,32]{1,0:T(1,128)} %bitcast.11), kind=kLoop, calls=%fused_computation.3 | loop fusion | flops 384 | bytes 1152 | tf_op jit(solution)/shard_map/concatenate | solution.py:645
  1.9 0.7 select_reduce_fusion.inv_ref
  2.6 101.3 %ffn.1 = (bf16[32,512]{1,0:T(8,128)(2,1)}, bf16[32,512]{1,0:T(8,128)(2,1)}, f32[2,2,16,64,128]{4,3,2,1,0:T(8,128)}, bf16[2,16,64,128]{3,2,1,0:T(8,128)(2,1)}, f32[32,64,128]{2,1,0:T(8,128)}) custom-call(s32[3,32]{1,0:T(4,128)} %get-tuple-element.26.slots_ref, s32[3,64]{1,0:T(4,128)} %select_reduce_fusion.inv_ref, bf16[32,512]{1,0:T(8,128)(2,1)} %tok_in.1, ...), custom_call_target="tpu_custom_call" | custom-call | flops 4831838208 | bytes 8388608 | tf_op jit(solution)/shard_map/ffn/pallas_call | solution.py:724
  103.9 4.4 %finish.1 = (bf16[32,512]{1,0:T(8,128)(2,1)}, bf16[32,512]{1,0:T(8,128)(2,1)}, f32[2,16,64,128]{3,2,1,0:T(8,128)}, f32[2,16,64,128]{3,2,1,0:T(8,128)}, f32[32,64,128]{2,1,0:T(8,128)}) custom-call(bf16[32,512]{1,0:T(8,128)(2,1)} %get-tuple-element.15.layer, bf16[32,512]{1,0:T(8,128)(2,1)} %get-tuple-element.16.tgrad, ...), custom_call_target="tpu_custom_call" | custom-call | tf_op jit(solution)/shard_map/finish/pallas_call | solution.py:740

commit v4 on v3

--- a/solution.py
+++ b/solution.py
@@ -11,7 +11,7 @@
 BLK = 128
 HB = BLK // 2
 UNITS = 2
-GRID = 4
+GRID = 2
 MESH = pl.DeviceIdType.MESH
 F32 = jnp.float32
 BF16 = jnp.bfloat16
@@ -237,21 +237,25 @@
     def z_rows(t):
         return al(lax.rem(t + 2 * nz, nz) * zrows, zrows)
 
-    def unit_rows(u, target):
-        if u == 0:
+    def split(t, u):
+        return u == 1 and t < 2
+
+    def unit_rows(t, u, target):
+        if not split(t, u):
             return z_rows(target)
         return al(z_rows(target) + yh * own_rows, own_rows)
 
-    count = (zrows, own_rows)
+    def count(t, u):
+        return own_rows if split(t, u) else zrows
 
     def rs_ref(buf, t, u, d, k):
         cs = pl.ds(d * half, half) if k == 0 else pl.ds(0, cw)
-        return buf.at[t, u, d, k, pl.ds(0, count[u]), cs]
+        return buf.at[t, u, d, k, pl.ds(0, count(t, u)), cs]
 
     def rs_start(t, u, d, k):
         target = z + (steps - k) * (1 - 2 * d)
-        rs = pl.ds(unit_rows(u, target), count[u])
-        to = pl.ds(0, count[u])
+        rs = pl.ds(unit_rows(t, u, target), count(t, u))
+        to = pl.ds(0, count(t, u))
         for h in range(2):
             if k == 0 and h != d:
                 continue
@@ -316,7 +320,6 @@
     for d in range(2):
         rs_start(2, 0, d, 0)
     product(2, 1)
-    yb_start(2)
 
     mine_r = al(z * zrows + yh * own_rows, own_rows)
     theirs_r = al(z * zrows + (1 - yh) * own_rows, own_rows)
@@ -331,27 +334,29 @@
     def rs_finish(t, u):
         for d in range(2):
             rs_wait(t, u, d, steps - 1)
-        if u == 0:
-            y_send[t] = last_sum(t, u, theirs_r, theirs_o).astype(BF16)
-            y_own[u, t] = last_sum(t, u, mine_r, mine_o)
-            if t == 2:
-                send(y_send, y_recv, ys_s.at[0], ys_r.at[0], y_dev)
-        else:
+        if split(t, u):
             y_own[u, t] = last_sum(t, u, mine_r, 0)
+            return
+        m = t + u
+        y_send[m] = last_sum(t, u, theirs_r, theirs_o).astype(BF16)
+        y_own[u, t] = last_sum(t, u, mine_r, mine_o)
+        if t == 2:
+            part_of = pl.ds(0, 3) if u == 0 else pl.ds(3, 1)
+            send(y_send.at[part_of], y_recv.at[part_of], ys_s.at[u], ys_r.at[u], y_dev)
 
     def rows_ref(r0, u):
         return act.at[:, pl.ds(r0, own_rows), pl.ds(u * cw, cw)]
 
     def activate(u):
-        if u == 0:
-            arrived(y_recv, ys_s.at[0], ys_r.at[0], y_dev)
+        part_of = pl.ds(0, 3) if u == 0 else pl.ds(3, 1)
+        arrived(y_recv.at[part_of], ys_s.at[u], ys_r.at[u], y_dev)
         for q in range(2):
             cs = pl.ds(q * half, half)
             gate, up, grad = (y_own[u, t, :, cs] for t in range(3))
             if u == 0:
                 gate = gate + y_recv[0, :, cs].astype(F32)
                 up = up + y_recv[1, :, cs].astype(F32)
-                grad = grad + y_recv[2, :, cs].astype(F32)
+            grad = grad + y_recv[2 + u, :, cs].astype(F32)
             sg = 1.0 / (1.0 + jnp.exp(-gate))
             co = pl.ds(u * cw + q * half, half)
             act[0, pl.ds(mine_r, own_rows), co] = (
@@ -363,7 +368,8 @@
         if u == 0:
             send(ref, ref, ay_s.at[0, steps], ay_r.at[0, steps], y_dev)
         else:
-            send(ref, ref, ya_s.at[0], ya_r.at[0], y_dev)
+            for t in range(3):
+                send(ref.at[t], ref.at[t], ya_s.at[t], ya_r.at[t], y_dev)
 
     def az_chunk(d, k, hops, hi):
         rs = pl.ds(al(z_rows(z - hops * (1 - 2 * d)) + hi * own_rows, own_rows), own_rows)
@@ -543,61 +549,66 @@
     def at(s, f, *a):
         slots.setdefault(s, []).append(functools.partial(f, *a))
 
-    def y_arrived():
-        arrived(rows_ref(theirs_r, 1), ya_s.at[0], ya_r.at[0], y_dev)
+    def y_arrived(t):
+        arrived(rows_ref(theirs_r, 1).at[t], ya_s.at[t], ya_r.at[t], y_dev)
 
     def tok_transpose():
         tok_t[...] = tcg[0].astype(F32).T.astype(BF16)
+
+    def start_last():
+        for d in range(2):
+            rs_start(2, 1, d, 0)
 
     for k in range(1, S):
         for t in range(3):
             at(k, rs_step, t, 0, k)
+    at(S - 2, start_last)
+    at(S - 2, tok_transpose)
+    at(S - 1, rs_step, 2, 1, 1)
     at(S - 1, yb_add, 0)
     at(S - 1, yb_add, 1)
     for t in range(3):
         at(S, rs_finish, t, 0)
-    at(S, rs_step, 0, 1, 1)
-    at(S, rs_step, 1, 1, 1)
-    at(S, yb_add, 2)
+    for k in range(1, S):
+        at(S - 1 + k, rs_step, 0, 1, k)
+        at(S - 1 + k, rs_step, 1, 1, k)
+    for k in range(2, S):
+        at(S - 2 + k, rs_step, 2, 1, k)
     at(S + 1, activate, 0)
+    at(2 * S - 2, rs_finish, 2, 1)
+    at(2 * S - 1, rs_finish, 0, 1)
+    at(2 * S - 1, rs_finish, 1, 1)
+    at(2 * S - 1, activate, 1)
+    for t in range(3):
+        for k in range(S + 1):
+            if k == 0:
+                at(2 * S + t, y_arrived, t)
+            at(2 * S + t + k, ag_step, t, k)
     for k in range(S + 1):
         at(S + 1 + k, az_step, k)
-    for k in range(2, S):
-        at(S - 1 + k, rs_step, 0, 1, k)
-        at(S - 1 + k, rs_step, 1, 1, k)
-    for k in range(1, S):
-        at(S + k, rs_step, 2, 1, k)
-    at(2 * S - 1, tok_transpose)
-    for t in range(3):
-        at(2 * S, rs_finish, t, 1)
-    at(2 * S, activate, 1)
-    at(2 * S + 1, y_arrived)
-    for k in range(S + 1):
-        at(2 * S + 1 + k, ag_step, 0, k)
-        at(2 * S + 1 + k, ag_step, 1, k)
-        at(2 * S + 2 + k, ag_step, 2, k)
-    A = 3 * S
+    A = 3 * S - 1
     at(A, ay_wait)
     at(A, wide_dense, 0, 0)
     at(A, wide_dense, 1, 0)
     at(A, grad_product, 0)
-    A = 3 * S + 1
+    A = 3 * S
     at(A, wide_dense, 0, 1)
     at(A, emit_wide, 0)
+    at(A, layer_product, 0)
+    at(A, transpose_hidden, 0)
+    A = 3 * S + 1
+    at(A, wide_dense, 1, 1)
+    at(A, emit_wide, 1)
     at(A, grad_product, 1)
     at(A, col_first, 1)
-    at(A, wide_dense, 1, 1)
-    at(A, emit_wide, 1)
+    at(A, down_dense, 0)
     at(A, col_second, 1)
-    at(A, layer_product, 0)
-    at(A, transpose_hidden, 0)
-    at(A, down_dense, 0)
-    at(A, col_third, 1)
     A = 3 * S + 2
     at(A, layer_product, 1)
     at(A, col_first, 0)
     at(A, transpose_hidden, 1)
     at(A, col_second, 0)
+    at(A, col_third, 1)
     at(A, down_dense, 1)
     at(A, emit_down)
     at(A, col_third, 0)
@@ -663,11 +674,11 @@
         vm((3, group, hid), F32),
         vm((3, UNITS, 2, steps, zrows, cw), BF16),
         vm((3, UNITS, 2, steps, zrows, cw), BF16),
-        vm((3, own_rows, cw), BF16),
-        vm((3, own_rows, cw), BF16),
+        vm((4, own_rows, cw), BF16),
+        vm((4, own_rows, cw), BF16),
         vm((UNITS, 3, own_rows, cw), F32),
-        vm((3, nz, own_rows, cw), BF16),
-        vm((3, nz, own_rows, cw), BF16),
+        vm((2, nz, own_rows, cw), BF16),
+        vm((2, nz, own_rows, cw), BF16),
         vm((3, group, hid), BF16),
         vm((width, group), BF16),
         vm((hid, group), BF16),
@@ -692,12 +703,12 @@
         dma((2, 3 * nx - 1)),
         dma((3, UNITS, 2, steps)),
         dma((3, UNITS, 2, steps)),
-        dma((1,)),
-        dma((1,)),
+        dma((2,)),
+        dma((2,)),
+        dma((2,)),
+        dma((2,)),
         dma((3,)),
         dma((3,)),
-        dma((1,)),
-        dma((1,)),
         dma((2, steps)),
         dma((2, steps)),
         dma((2, steps + 1)),

time: 109 us -> 103 us (0.945)
  Pallas kernels: 106 us -> 99.7 us
    pallas_call x1, Pallas kernels: 101 us -> 96.3 us  [per_device(): pl.pallas_call(functools.partial(kernel, dims), out_shape=inner, in_specs...]
where the time goes in v4:
time: 103 us; the launch traced here: 102 us
  Pallas kernels  99.7 us (97%)
  other arithmetic  1.95 us (2%)
    pallas_call x1, Pallas kernels, per_device(): pl.pallas_call(functools.partial(kernel, dims), out_shape=inner, in_specs...  96.3 us
    pallas_call x1, Pallas kernels, per_device(): pl.pallas_call(finish, grid=(GRID,), out_shape=(inner[0], inner[1], jax.S...  3.37 us

profile of v4, /device:TPU:8, one launch (start us, length us, event | category | flops | bytes accessed | tf_op | source)
XLA Modules:
  0.0 102.3 jit_solution(8169093702420930656)
XLA Ops:
  0.6 1.3 %pad_add_fusion = (s32[3,32]{1,0:T(4,128)S(1)}, s32[3,32]{1,0:T(4,128)}) fusion(s32[1,32]{1,0:T(1,128)} %bitcast.9, s32[1,32]{1,0:T(1,128)} %bitcast.10, s32[1,32]{1,0:T(1,128)} %bitcast.11), kind=kLoop, calls=%fused_computation.3 | loop fusion | flops 384 | bytes 1152 | tf_op jit(solution)/shard_map/concatenate | solution.py:656
  1.9 0.7 select_reduce_fusion.inv_ref
  2.6 96.3 %ffn.1 = (bf16[32,512]{1,0:T(8,128)(2,1)}, bf16[32,512]{1,0:T(8,128)(2,1)}, f32[2,2,16,64,128]{4,3,2,1,0:T(8,128)}, bf16[2,16,64,128]{3,2,1,0:T(8,128)(2,1)}, f32[32,64,128]{2,1,0:T(8,128)}) custom-call(s32[3,32]{1,0:T(4,128)} %get-tuple-element.26.slots_ref, s32[3,64]{1,0:T(4,128)} %select_reduce_fusion.inv_ref, bf16[32,512]{1,0:T(8,128)(2,1)} %tok_in.1, ...), custom_call_target="tpu_custom_call" | custom-call | flops 4831838208 | bytes 8388608 | tf_op jit(solution)/shard_map/ffn/pallas_call | solution.py:735
  98.9 3.4 %finish.1 = (bf16[32,512]{1,0:T(8,128)(2,1)}, bf16[32,512]{1,0:T(8,128)(2,1)}, f32[2,16,64,128]{3,2,1,0:T(8,128)}, f32[2,16,64,128]{3,2,1,0:T(8,128)}, f32[32,64,128]{2,1,0:T(8,128)}) custom-call(bf16[32,512]{1,0:T(8,128)(2,1)} %get-tuple-element.15.layer, bf16[32,512]{1,0:T(8,128)(2,1)} %get-tuple-element.16.tgrad, ...), custom_call_target="tpu_custom_call" | custom-call | tf_op jit(solution)/shard_map/finish/pallas_call | solution.py:751

commit v5 on v4

--- a/solution.py
+++ b/solution.py
@@ -580,10 +580,10 @@
     at(2 * S - 1, rs_finish, 1, 1)
     at(2 * S - 1, activate, 1)
     for t in range(3):
+        lag = 2 * S + (t == 2)
+        at(lag, y_arrived, t)
         for k in range(S + 1):
-            if k == 0:
-                at(2 * S + t, y_arrived, t)
-            at(2 * S + t + k, ag_step, t, k)
+            at(lag + k, ag_step, t, k)
     for k in range(S + 1):
         at(S + 1 + k, az_step, k)
     A = 3 * S - 1
@@ -594,21 +594,20 @@
     A = 3 * S
     at(A, wide_dense, 0, 1)
     at(A, emit_wide, 0)
-    at(A, layer_product, 0)
-    at(A, transpose_hidden, 0)
-    A = 3 * S + 1
     at(A, wide_dense, 1, 1)
     at(A, emit_wide, 1)
     at(A, grad_product, 1)
     at(A, col_first, 1)
-    at(A, down_dense, 0)
+    at(A, layer_product, 0)
     at(A, col_second, 1)
-    A = 3 * S + 2
+    A = 3 * S + 1
     at(A, layer_product, 1)
     at(A, col_first, 0)
+    at(A, transpose_hidden, 0)
     at(A, transpose_hidden, 1)
     at(A, col_second, 0)
     at(A, col_third, 1)
+    at(A, down_dense, 0)
     at(A, down_dense, 1)
     at(A, emit_down)
     at(A, col_third, 0)

time: 103 us -> 100 us (0.971)
  Pallas kernels: 99.7 us -> 97.1 us
    pallas_call x1, Pallas kernels: 96.3 us -> 93.7 us  [per_device(): pl.pallas_call(functools.partial(kernel, dims), out_shape=inner, in_specs...]
where the time goes in v5:
time: 100 us; the launch traced here: 99.7 us
  Pallas kernels  97.1 us (97%)
  other arithmetic  1.95 us (2%)
    pallas_call x1, Pallas kernels, per_device(): pl.pallas_call(functools.partial(kernel, dims), out_shape=inner, in_specs...  93.7 us
    pallas_call x1, Pallas kernels, per_device(): pl.pallas_call(finish, grid=(GRID,), out_shape=(inner[0], inner[1], jax.S...  3.37 us

profile of v5, /device:TPU:8, one launch (start us, length us, event | category | flops | bytes accessed | tf_op | source)
XLA Modules:
  0.0 99.7 jit_solution(13763706182650344559)
XLA Ops:
  0.6 1.3 %pad_add_fusion = (s32[3,32]{1,0:T(4,128)S(1)}, s32[3,32]{1,0:T(4,128)}) fusion(s32[1,32]{1,0:T(1,128)} %bitcast.9, s32[1,32]{1,0:T(1,128)} %bitcast.10, s32[1,32]{1,0:T(1,128)} %bitcast.11), kind=kLoop, calls=%fused_computation.3 | loop fusion | flops 384 | bytes 1152 | tf_op jit(solution)/shard_map/concatenate | solution.py:655
  1.9 0.7 select_reduce_fusion.inv_ref
  2.6 93.7 %ffn.1 = (bf16[32,512]{1,0:T(8,128)(2,1)}, bf16[32,512]{1,0:T(8,128)(2,1)}, f32[2,2,16,64,128]{4,3,2,1,0:T(8,128)}, bf16[2,16,64,128]{3,2,1,0:T(8,128)(2,1)}, f32[32,64,128]{2,1,0:T(8,128)}) custom-call(s32[3,32]{1,0:T(4,128)} %get-tuple-element.26.slots_ref, s32[3,64]{1,0:T(4,128)} %select_reduce_fusion.inv_ref, bf16[32,512]{1,0:T(8,128)(2,1)} %tok_in.1, ...), custom_call_target="tpu_custom_call" | custom-call | flops 4831838208 | bytes 8388608 | tf_op jit(solution)/shard_map/ffn/pallas_call | solution.py:734
  96.3 3.4 %finish.1 = (bf16[32,512]{1,0:T(8,128)(2,1)}, bf16[32,512]{1,0:T(8,128)(2,1)}, f32[2,16,64,128]{3,2,1,0:T(8,128)}, f32[2,16,64,128]{3,2,1,0:T(8,128)}, f32[32,64,128]{2,1,0:T(8,128)}) custom-call(bf16[32,512]{1,0:T(8,128)(2,1)} %get-tuple-element.15.layer, bf16[32,512]{1,0:T(8,128)(2,1)} %get-tuple-element.16.tgrad, ...), custom_call_target="tpu_custom_call" | custom-call | tf_op jit(solution)/shard_map/finish/pallas_call | solution.py:750

commit v6 on v5

--- a/solution.py
+++ b/solution.py
@@ -39,7 +39,9 @@
 
 def kernel(
     dims,
-    slots_ref,
+    gate_slots,
+    up_slots,
+    down_slots,
     inv_ref,
     tok_in,
     cot_in,
@@ -206,7 +208,7 @@
     for i in range(3):
         blocks[i, cap] = jnp.zeros((BLK, BLK), BF16)
     for ref in (dense_g, dense_u, dense_d):
-        ref[drb * fcb] = jnp.zeros(ref.shape[1:], F32)
+        ref[0] = jnp.zeros(ref.shape[1:], F32)
 
     def place_wide(p, carry):
         r, c = p // (fcb // 2), p % (fcb // 2)
@@ -430,18 +432,19 @@
                     both = value[a * BLK : (a + 1) * BLK, b * BLK : (b + 1) * BLK]
                     turned = swap(both)
                     c = 4 * (u * per + j) + 2 * b
-                    dense[a * fcb + c] = jnp.where(low, both, turned)
-                    dense[a * fcb + c + 1] = jnp.where(low, turned, both)
+                    dense[a * fcb + c + 1] = jnp.where(low, both, turned)
+                    dense[a * fcb + c + 2] = jnp.where(low, turned, both)
             return carry
 
         lax.fori_loop(0, per, body, 0)
 
     def emit_wide(i):
         dense = (dense_g, dense_u)[i]
+        slot_list = (gate_slots, up_slots)[i]
 
         def body(s, carry):
-            one = dense[slots_ref[i, s]]
-            two = dense[slots_ref[i, s + cap // 2]]
+            one = dense[slot_list[0, s] + 1]
+            two = dense[slot_list[0, s + cap // 2] + 1]
             lanes = lane_half(HB)
             for h, value in enumerate((one, two)):
                 keep = jnp.where(dp == 0, value[:HB], value[HB:])
@@ -470,7 +473,7 @@
             value = dot(hid_t[pl.ds(al(u * cw + j * 256, 256), 256), :], tcg[1])
             for a in range(4):
                 for b in range(drb):
-                    dense_d[(4 * (u * per + j) + a) * drb + b] = value[
+                    dense_d[(4 * (u * per + j) + a) * drb + b + 1] = value[
                         a * HB : (a + 1) * HB, b * BLK : (b + 1) * BLK
                     ]
             return carry
@@ -479,7 +482,7 @@
 
     def emit_down():
         def body(s, carry):
-            down_own[s] = dense_d[slots_ref[2, s]]
+            down_own[s] = dense_d[down_slots[0, s] + 1]
             return carry
 
         lax.fori_loop(0, cap, body, 0)
@@ -606,10 +609,10 @@
     at(A, transpose_hidden, 0)
     at(A, transpose_hidden, 1)
     at(A, col_second, 0)
-    at(A, col_third, 1)
     at(A, down_dense, 0)
     at(A, down_dense, 1)
     at(A, emit_down)
+    at(A, col_third, 1)
     at(A, col_third, 0)
     at(A, col_last, 1, tgrad_out)
     at(A, col_last, 0, layer_out)
@@ -658,7 +661,6 @@
     inv = jnp.min(
         jnp.where(slots[:, None, :] == place[None, :, None], order[None, None, :], cap), axis=2
     )
-    slots = jnp.where(slots < 0, drb * fcb, slots)
     dims = (n_row, n_col, n_tok, width, hid, cap)
     smem = pl.BlockSpec(memory_space=pltpu.SMEM)
     anym = pl.BlockSpec(memory_space=pl.ANY)
@@ -734,7 +736,7 @@
     results = pl.pallas_call(
         functools.partial(kernel, dims),
         out_shape=inner,
-        in_specs=[smem, smem, anym, anym, anym, anym, anym],
+        in_specs=[smem, smem, smem, smem, anym, anym, anym, anym, anym],
         out_specs=(anym,) * 5,
         scratch_shapes=scratch,
         compiler_params=pltpu.CompilerParams(
@@ -742,7 +744,7 @@
         ),
         cost_estimate=pl.CostEstimate(flops=flops, bytes_accessed=8 * 1024 * 1024, transcendentals=0),
         name="ffn",
-    )(slots, inv, tokens, cotangent, gate_blocks[0, 0], up_blocks[0, 0], down_blocks[0, 0])
+    )(gate_slots[0], up_slots[0], down_slots[0], inv, tokens, cotangent, gate_blocks[0, 0], up_blocks[0, 0], down_blocks[0, 0])
     ns = cap // 2 // GRID
     flat = pl.BlockSpec((n_tok, width), lambda g: (0, 0))
     wide = pl.BlockSpec((2, ns, HB, BLK), lambda g: (0, g, 0, 0))

time: 100 us -> 99.7 us (level)
  no operation moved by 1% of the time
where the time goes in v6:
time: 99.7 us; the launch traced here: 99.1 us
  Pallas kernels  97.1 us (97%)
  other arithmetic  1.37 us (1%)
    pallas_call x1, Pallas kernels, per_device(): pl.pallas_call(functools.partial(kernel, dims), out_shape=inner, in_specs...  93.7 us
    pallas_call x1, Pallas kernels, per_device(): pl.pallas_call(finish, grid=(GRID,), out_shape=(inner[0], inner[1], jax.S...  3.37 us

profile of v6, /device:TPU:8, one launch (start us, length us, event | category | flops | bytes accessed | tf_op | source)
XLA Modules:
  0.0 99.1 jit_solution(17386577554420750065)
XLA Ops:
  0.6 0.7 pad_add_fusion
  1.3 0.7 select_reduce_fusion.inv_ref
  2.0 93.7 %ffn.1 = (bf16[32,512]{1,0:T(8,128)(2,1)}, bf16[32,512]{1,0:T(8,128)(2,1)}, f32[2,2,16,64,128]{4,3,2,1,0:T(8,128)}, bf16[2,16,64,128]{3,2,1,0:T(8,128)(2,1)}, f32[32,64,128]{2,1,0:T(8,128)}) custom-call(s32[1,32]{1,0:T(1,128)} %bitcast.10, s32[1,32]{1,0:T(1,128)} %bitcast.12, s32[1,32]{1,0:T(1,128)} %bitcast.14, s32[3,64]{1,0:T(4,128)} %select_reduce_fusion.inv_ref, ...), custom_call_target="tpu_custom_call" | custom-call | flops 4831838208 | bytes 8388608 | tf_op jit(solution)/shard_map/ffn/pallas_call | solution.py:736
  95.7 3.4 %finish.1 = (bf16[32,512]{1,0:T(8,128)(2,1)}, bf16[32,512]{1,0:T(8,128)(2,1)}, f32[2,16,64,128]{3,2,1,0:T(8,128)}, f32[2,16,64,128]{3,2,1,0:T(8,128)}, f32[32,64,128]{2,1,0:T(8,128)}) custom-call(bf16[32,512]{1,0:T(8,128)(2,1)} %get-tuple-element.15.layer, bf16[32,512]{1,0:T(8,128)(2,1)} %get-tuple-element.16.tgrad, ...), custom_call_target="tpu_custom_call" | custom-call | tf_op jit(solution)/shard_map/finish/pallas_call | solution.py:752

commit v7 on v6

--- a/solution.py
+++ b/solution.py
@@ -315,8 +315,7 @@
             rs_start(t, 0, d, 0)
         product(t, 1)
         yb_start(t)
-        if t == 0:
-            gather_pass(1)
+    gather_pass(1)
     gather_end(1)
     product(2, 0)
     for d in range(2):

time: 99.7 us -> 100 us (level)
  no operation moved by 1% of the time
where the time goes in v7:
time: 100 us; the launch traced here: 99.1 us
  Pallas kernels  97.1 us (97%)
  other arithmetic  1.37 us (1%)
    pallas_call x1, Pallas kernels, per_device(): pl.pallas_call(functools.partial(kernel, dims), out_shape=inner, in_specs...  93.7 us
    pallas_call x1, Pallas kernels, per_device(): pl.pallas_call(finish, grid=(GRID,), out_shape=(inner[0], inner[1], jax.S...  3.37 us

profile of v7, /device:TPU:8, one launch (start us, length us, event | category | flops | bytes accessed | tf_op | source)
XLA Modules:
  0.0 99.1 jit_solution(9935137493451827067)
XLA Ops:
  0.6 0.7 pad_add_fusion
  1.3 0.7 select_reduce_fusion.inv_ref
  2.0 93.7 %ffn.1 = (bf16[32,512]{1,0:T(8,128)(2,1)}, bf16[32,512]{1,0:T(8,128)(2,1)}, f32[2,2,16,64,128]{4,3,2,1,0:T(8,128)}, bf16[2,16,64,128]{3,2,1,0:T(8,128)(2,1)}, f32[32,64,128]{2,1,0:T(8,128)}) custom-call(s32[1,32]{1,0:T(1,128)} %bitcast.10, s32[1,32]{1,0:T(1,128)} %bitcast.12, s32[1,32]{1,0:T(1,128)} %bitcast.14, s32[3,64]{1,0:T(4,128)} %select_reduce_fusion.inv_ref, ...), custom_call_target="tpu_custom_call" | custom-call | flops 4831838208 | bytes 8388608 | tf_op jit(solution)/shard_map/ffn/pallas_call | solution.py:735
  95.7 3.4 %finish.1 = (bf16[32,512]{1,0:T(8,128)(2,1)}, bf16[32,512]{1,0:T(8,128)(2,1)}, f32[2,16,64,128]{3,2,1,0:T(8,128)}, f32[2,16,64,128]{3,2,1,0:T(8,128)}, f32[32,64,128]{2,1,0:T(8,128)}) custom-call(bf16[32,512]{1,0:T(8,128)(2,1)} %get-tuple-element.15.layer, bf16[32,512]{1,0:T(8,128)(2,1)} %get-tuple-element.16.tgrad, ...), custom_call_target="tpu_custom_call" | custom-call | tf_op jit(solution)/shard_map/finish/pallas_call | solution.py:751
